TPU v7x, 128 devices: a whole 4x4x4 slice. The times are simulated.
128 devices in a mesh: lat: 64 (over x, z, y_lo, core), lon: 2 (over y_hi).
Axes of the slice: x: 4, y: 4 (y_hi: 2, y_lo: 2; y = y_hi * 2 + y_lo), z: 4, core: 2. Of those that a mesh axis runs over, the one named last changes fastest.
Arguments:
- grid_field: bfloat16 [384, 1440, 512], P('lat', 'lon'), may hold values from -6 to 6
- disco_taps: float32 [3, 384, 3, 5], P(None, 'lat'), may hold values from -1.5 to 1.5
- disco_mix: bfloat16 [1536, 512], replicated, may hold values from -0.15625 to 0.15625
- legendre: bfloat16 [256, 256, 384], P('lat'), may hold values from -0.3125 to 0.3125
- quad_weights: float32 [384], P('lat'), may hold values from 0.5 to 2
- mix_weight: bfloat16 [2, 512, 512], replicated, may hold values from -0.1875 to 0.1875
- degree_gain: float32 [256, 512], replicated, may hold values from 0.5 to 2
Outputs:
- block_output: bfloat16 [384, 1440, 512], P('lat', 'lon')
All inputs are finite; a program needn't handle non-finite values.
Results may differ from a plain program's by a relative error of at most 0.018.
Values may be sent and summed in bfloat16 or wider, within the bound.
A program may use at most 320 MiB of HBM per device.

v0:
```python
import math

import jax
import jax.numpy as jnp
from jax import lax
from jax.sharding import PartitionSpec as P

MODES = 256


def padded_2(x, sides, width, wrap):
    for axis, dim in sides:
        peers, length = (lax.axis_size(axis), x.shape[dim])
        up = [(i, (i + 1) % peers) for i in range(peers if wrap else peers - 1)]
        down = [(j, i) for i, j in up]
        last = lax.slice_in_dim(x, length - width, length, axis=dim)
        first = lax.slice_in_dim(x, 0, width, axis=dim)
        before = lax.ppermute(last, axis, up)
        after = lax.ppermute(first, axis, down)
        x = jnp.concatenate([before, x, after], axis=dim)
    return x


def dft_basis(offset, number, length, mode_count):
    longitudes = offset + jnp.arange(number, dtype=jnp.int32)
    orders = jnp.arange(mode_count, dtype=jnp.int32)
    product = longitudes[:, None] * orders[None, :] % length
    angles = product.astype(jnp.float32) * (2.0 * math.pi / length)
    paired = jnp.stack([jnp.cos(angles), -jnp.sin(angles)], axis=2) * (1.0 / math.sqrt(length))
    return paired.reshape(number, 2 * mode_count).astype(jnp.bfloat16)


def triangle_table(legendre, first_mode):
    mode_count = legendre.shape[0]
    degree_count = legendre.shape[1]
    orders = first_mode + jnp.arange(mode_count, dtype=jnp.int32)
    degrees = jnp.arange(degree_count, dtype=jnp.int32)
    keep = degrees[None, :, None] >= orders[:, None, None]
    return jnp.where(keep, legendre, jnp.zeros_like(legendre))


def mixing_matrix(real_part, imag_part):
    upper = jnp.concatenate([real_part, imag_part], axis=1)
    lower = jnp.concatenate([-imag_part, real_part], axis=1)
    return jnp.concatenate([upper, lower], axis=0)


def body(grid_field, disco_taps, disco_mix, legendre, quad_weights, mix_weight, degree_gain):
    cycle_count, lon_count, channels = grid_field.shape
    kernels = disco_taps.shape[0]
    lon_size = lax.axis_size("lon")
    lon_place = lax.axis_index("lon")
    lat_place = lax.axis_index("lat")
    own_channels = channels // lon_size
    full_length = lon_count * lon_size
    channel_start = lon_place * own_channels
    widened = padded_2(grid_field, (("lon", 1),), 2, True)
    padded = padded_2(widened, (("lat", 0),), 1, False)
    summed = jnp.zeros((kernels, cycle_count, lon_count, channels), jnp.float32)
    for row_shift in range(3):
        for col_shift in range(5):
            shifted = padded[
                row_shift : row_shift + cycle_count, col_shift : col_shift + lon_count, :
            ]
            summed = summed + disco_taps[:, :, row_shift, col_shift][:, :, None, None] * shifted[
                None
            ].astype(jnp.float32)
    basis_terms = summed.astype(jnp.bfloat16)
    conv_weight = disco_mix.reshape(kernels, channels, channels)
    conv = jnp.einsum(
        "kijc,kco->ijo", basis_terms, conv_weight, preferred_element_type=jnp.float32
    ).astype(jnp.bfloat16)
    own_table = dft_basis(lon_place * lon_count, lon_count, full_length, MODES)
    partial_terms = jnp.einsum("jq,ijc->iqc", own_table, conv, preferred_element_type=jnp.float32)
    spectrum = lax.psum_scatter(
        partial_terms.astype(jnp.bfloat16), "lon", scatter_dimension=2, tiled=True
    ).astype(jnp.float32)
    weighted = (spectrum * quad_weights[:, None, None]).astype(jnp.bfloat16)
    mode_local = legendre.shape[0]
    degree_count = legendre.shape[1]
    triangle = triangle_table(legendre, lat_place * mode_local)
    regrouped = lax.all_to_all(weighted, "lat", split_axis=1, concat_axis=0, tiled=True)
    split_parts = regrouped.reshape(regrouped.shape[0], mode_local, 2, regrouped.shape[2])
    coeffs = jnp.einsum(
        "mli,impc->mlpc", triangle, split_parts, preferred_element_type=jnp.float32
    ).astype(jnp.bfloat16)
    own_gain = lax.dynamic_slice_in_dim(degree_gain, channel_start, own_channels, 1)
    gathered = lax.all_gather(coeffs, "lon", axis=3, tiled=True)
    real_cols = lax.dynamic_slice_in_dim(mix_weight[0], channel_start, own_channels, 1)
    imag_cols = lax.dynamic_slice_in_dim(mix_weight[1], channel_start, own_channels, 1)
    block_weight = mixing_matrix(real_cols, imag_cols)
    flattened = gathered.reshape(mode_local * degree_count, 2 * channels)
    mixed_sum = jnp.dot(flattened, block_weight, preferred_element_type=jnp.float32)
    mixed_sum = mixed_sum.reshape(mode_local, degree_count, 2, own_channels)
    mixed_modes = (mixed_sum * own_gain[None, :, None, :]).astype(jnp.bfloat16)
    synth = jnp.einsum(
        "mli,mlpc->impc", triangle, mixed_modes, preferred_element_type=jnp.float32
    ).astype(jnp.bfloat16)
    synth = synth.reshape(synth.shape[0], 2 * mode_local, own_channels)
    cycle_data = lax.all_to_all(synth, "lat", split_axis=0, concat_axis=1, tiled=True)
    returned = jnp.einsum(
        "jq,iqc->ijc",
        own_table,
        lax.all_gather(cycle_data, "lon", axis=2, tiled=True),
        preferred_element_type=jnp.float32,
    )
    return (conv.astype(jnp.float32) + returned).astype(jnp.bfloat16)


def solution(mesh):
    return jax.shard_map(
        body,
        mesh=mesh,
        in_specs=(
            P("lat", "lon", None),
            P(None, "lat", None, None),
            P(),
            P("lat", None, None),
            P("lat"),
            P(),
            P(),
        ),
        out_specs=P("lat", "lon", None),
        check_vma=False,
    )
```

profile of v0, /device:TPU:1, one launch (start us, length us, event | category | flops | bytes accessed | tf_op | source)
XLA Modules:
  0.0 401.5 jit_solution(1928487859580180844)
XLA Ops:
  7.5 3.8 collective-permute-start.1
  12.3 3.1 fusion.45
  18.6 3.1 pad_maximum_fusion.4
  21.8 4.3 %collective-permute-start.2 = (bf16[1,724,512]{2,1,0:T(8,128)(2,1)}, bf16[1,724,512]{2,1,0:T(8,128)(2,1)S(1)}, u32[]{:S(2)}, u32[]{:S(2)}) collective-permute-start(bf16[1,724,512]{2,1,0:T(8,128)(2,1)} %get-tuple-element.21), channel_id=1, source_target_pairs={{0,2},{2,4},{4,6},{6,8},{8,10},{10,12},{12,14},{14,16},{16,18},{18... | collective-permute-start | bytes 2224136 | tf_op jit(solution)/shard_map/ppermute | solution.py:18
  26.0 2.1 collective-permute-start.3
  28.2 11.4 %fusion.33 = (f32[6,720,512]{2,1,0:T(8,128)}, f32[6,720,512]{2,1,0:T(8,128)}, bf16[6,722,512]{2,1,0:T(8,128)(2,1)}, f32[6,720,512]{2,1,0:T(8,128)}) fusion(bf16[6,2,512]{2,1,0:T(2,128)(2,1)S(1)} %collective-permute-done, bf16[6,720,512]{2,1,0:T(8,128)(2,1)S(1)} %copy-done.2), kind=kLoop, calls=%fused_computation.40 | loop fusion | flops 19906560 | bytes 35401728 | tf_op jit(solution)/shard_map/convert_element_type | solution.py:67
  40.1 12.4 %slice_convert_fusion.6 = (f32[6,720,512]{2,1,0:T(8,128)}, f32[6,720,512]{2,1,0:T(8,128)}) fusion(bf16[6,722,512]{2,1,0:T(8,128)(2,1)} %constant_dynamic-update-slice_fusion), kind=kLoop, calls=%fused_computation.47 | loop fusion | flops 4423680 | bytes 26542080 | tf_op jit(solution)/shard_map/convert_element_type | solution.py:67
  52.5 11.9 %maximum_maximum_fusion = (bf16[7,724,512]{2,1,0:T(8,128)(2,1)}, bf16[7,724,512]{2,1,0:T(8,128)(2,1)}) fusion(bf16[6,2,512]{2,1,0:T(2,128)(2,1)S(1)} %collective-permute-done.1, bf16[6,720,512]{2,1,0:T(8,128)(2,1)} %param.7, bf16[6,2,512]{2,1,0:T(2,128)(2,1)S(1)} %collective-permute-done, bf16[1,724,512]{2,1,0:T(8,128)(2,1)S(1)} %collective-permute-done.2, ...), kind=kLoop, calls=%fused_computation.35 | loop fusion | flops 41517056 | bytes 16310272 | tf_op jit(solution)/shard_map/concatenate | solution.py:20
  64.4 44.2 %slice_convert_fusion.4 = (f32[6,720,512]{2,1,0:T(8,128)}, f32[6,720,512]{2,1,0:T(8,128)}, f32[6,720,512]{2,1,0:T(8,128)}, f32[6,720,512]{2,1,0:T(8,128)}, f32[6...) fusion(bf16[7,724,512]{2,1,0:T(8,128)(2,1)} %get-tuple-element., ...), kind=kLoop, calls=%fused_computation.45 | loop fusion | flops 22118400 | bytes 132710400 | tf_op jit(solution)/shard_map/convert_element_type | solution.py:67
  108.6 46.6 %bitcast_convert_fusion = bf16[6,720,512]{2,1,0:T(8,128)(2,1)S(1)} fusion(bf16[3,512,512,1]{2,1,0,3:T(8,128)(2,1)S(1)} %bitcast.79, f32[6,720,512]{2,1,0:T(8,128)} %get-tuple-element.13, f32[3,6]{0,1:T(8,128)S(1)} %bitcast.85, f32[6,720,512]{2,1,0:T(8,128)} %get-tuple-element.14, f32[3,6]{0,1:T(8,128)S(1)} %bitcast.86, ...), kind=kOutput, calls=%fused_computation.34 | convolution fusion | flops 6996049920 | bytes 138708032 | tf_op jit(solution)/shard_map/kijc,kco->ijo/dot_general | solution.py:70
  157.3 4.2 %convert_bitcast_fusion = bf16[6,512,512]{1,2,0:T(8,128)(2,1)} fusion(bf16[6,720,512]{2,1,0:T(8,128)(2,1)S(1)} %bitcast_convert_fusion, bf16[720,512]{0,1:T(8,128)(2,1)S(1)} %convert_element_type.136), kind=kOutput, calls=%fused_computation.56 | convolution fusion | flops 2266497024 | bytes 8306688 | tf_op jit(solution)/shard_map/jq,ijc->iqc/dot_general | solution.py:74
  161.6 50.7 %reduce-scatter.2.cloned.1.call-done = bf16[6,512,256]{1,2,0:T(8,128)(2,1)} async-done(((bf16[6,512,512]{1,2,0:T(8,128)(2,1)}), bf16[6,512,256]{1,2,0:T(8,128)(2,1)}) %reduce-scatter.2.cloned.1.call-update) | async-done | bytes 1572880 | tf_op jit(solution)/shard_map/reduce_scatter | solution.py:75
  214.2 3.0 copy.120
  217.2 8.4 %all-to-all-start = ((bf16[6,512,256]{2,0,1:T(8,128)(2,1)}), bf16[6,512,256]{2,0,1:T(8,128)(2,1)}, u32[]{:S(2)}, u32[]{:S(2)}) async-start(bf16[6,512,256]{2,0,1:T(8,128)(2,1)} %copy.120), calls=%async_computation.1 | async-start | bytes 4194304 | tf_op jit(solution)/shard_map/all_to_all | solution.py:82
  225.8 28.8 %all-to-all-done = bf16[6,512,256]{2,0,1:T(8,128)(2,1)} async-done(((bf16[6,512,256]{2,0,1:T(8,128)(2,1)}), bf16[6,512,256]{2,0,1:T(8,128)(2,1)}, u32[]{:S(2)}, u32[]{:S(2)}) %all-to-all-start) | async-done | bytes 1572896 | tf_op jit(solution)/shard_map/all_to_all | solution.py:82
  254.5 3.1 copy.154
  257.6 2.6 reshape.183
  260.3 2.9 convolution_convert_fusion.1
  264.8 33.6 %all-gather.3.cloned.1.call-done = bf16[4,256,2,512]{3,1,2,0:T(8,128)(2,1)} async-done(((bf16[4,256,2,256]{3,1,2,0:T(8,128)(2,1)}), bf16[4,256,2,512]{3,1,2,0:T(8,128)(2,1)}) %all-gather.3.cloned.1.call-update) | async-done | bytes 2097168 | tf_op jit(solution)/shard_map/all_gather | solution.py:88
  298.4 4.1 %copy.124 = bf16[4,256,2,512]{1,3,2,0:T(8,128)(2,1)} copy(bf16[4,256,2,512]{3,1,2,0:T(8,128)(2,1)} %all-gather.3.cloned.1.call-done) | data formatting | bytes 4194304 | tf_op jit(solution)/shard_map/all_gather | solution.py:88
  302.5 4.0 convolution_convert_fusion
  307.9 31.4 %all_to_all.33 = bf16[384,8,256]{2,1,0:T(8,128)(2,1)S(1)} all-to-all(bf16[384,8,256]{2,1,0:T(8,128)(2,1)S(1)} %copy.128), channel_id=1, replica_groups=mesh['lat'=64,'lon'=2] {'lat'}, dimensions={0} | all-to-all | bytes 3145728 | tf_op jit(solution)/shard_map/all_to_all | solution.py:100
  340.6 46.0 %all-gather.5.cloned.1.call-done = bf16[6,512,512]{2,1,0:T(8,128)(2,1)} async-done(((bf16[6,512,256]{2,1,0:T(8,128)(2,1)}), bf16[6,512,512]{2,1,0:T(8,128)(2,1)}) %all-gather.5.cloned.1.call-update) | async-done | bytes 3145744 | tf_op jit(solution)/shard_map/all_gather | solution.py:104
  386.6 8.3 %fusion.31 = bf16[6,720,512]{2,1,0:T(8,128)(2,1)} fusion(bf16[6,720,512]{2,1,0:T(8,128)(2,1)} %copy-done.7, bf16[6,512,512]{2,1,0:T(8,128)(2,1)} %all-gather.5.cloned.1.call-done, bf16[720,512]{0,1:T(8,128)(2,1)} %copy-done.4), kind=kOutput, calls=%fused_computation.33 | convolution fusion | flops 2271559680 | bytes 12730368 | tf_op jit(solution)/shard_map/jq,iqc->ijc/dot_general | solution.py:101
  (60 shorter events, 14.1 us)
Async XLA Ops:
  6.5 102.0 %copy-start = (bf16[1536,512]{1,0:T(8,128)(2,1)S(1)}, bf16[1536,512]{1,0:T(8,128)(2,1)}, u32[]{:S(2)}) copy-start(bf16[1536,512]{1,0:T(8,128)(2,1)} %param.9) | copy-start | bytes 4718596
  6.5 205.7 %reduce-scatter.2.cloned.1.call-start = ((), (), s32[]{:S(2)}) async-start(), calls=%async_computation.3 | async-start | bytes 4718592 | tf_op jit(solution)/shard_map/reduce_scatter | solution.py:75
  7.5 11.1 %collective-permute-start.1 = (bf16[6,2,512]{2,1,0:T(2,128)(2,1)S(1)}, bf16[6,2,512]{2,1,0:T(2,128)(2,1)S(1)}, u32[]{:S(2)}, u32[]{:S(2)}) collective-permute-start(bf16[6,2,512]{2,1,0:T(2,128)(2,1)S(1)} %get-tuple-element.28), channel_id=1, source_target_pairs={{1,0},{0,1},{3,2},{2,3},{5,4},{4,5},{7,6},{6,7},{9,8},{8,9},{11,10... | collective-permute-start | bytes 36872 | tf_op jit(solution)/shard_map/ppermute | solution.py:19
  11.3 7.3 %collective-permute-start = (bf16[6,2,512]{2,1,0:T(2,128)(2,1)S(1)}, bf16[6,2,512]{2,1,0:T(2,128)(2,1)S(1)}, u32[]{:S(2)}, u32[]{:S(2)}) collective-permute-start(bf16[6,2,512]{2,1,0:T(2,128)(2,1)S(1)} %get-tuple-element.27), channel_id=1, source_target_pairs={{0,1},{1,0},{2,3},{3,2},{4,5},{5,4},{6,7},{7,6},{8,9},{9,8},{10,11... | collective-permute-start | bytes 36872 | tf_op jit(solution)/shard_map/ppermute | solution.py:18
  18.6 136.6 %copy-start.4 = (bf16[720,512]{0,1:T(8,128)(2,1)}, bf16[720,512]{0,1:T(8,128)(2,1)S(1)}, u32[]{:S(2)}) copy-start(bf16[720,512]{0,1:T(8,128)(2,1)S(1)} %convert_element_type.136) | copy-start | bytes 2211844
  18.6 9.5 %copy-start.2 = (bf16[6,720,512]{2,1,0:T(8,128)(2,1)S(1)}, bf16[6,720,512]{2,1,0:T(8,128)(2,1)}, u32[]{:S(2)}) copy-start(bf16[6,720,512]{2,1,0:T(8,128)(2,1)} %param.7) | copy-start | bytes 13271044
  21.8 30.8 %collective-permute-start.2 = (bf16[1,724,512]{2,1,0:T(8,128)(2,1)}, bf16[1,724,512]{2,1,0:T(8,128)(2,1)S(1)}, u32[]{:S(2)}, u32[]{:S(2)}) collective-permute-start(bf16[1,724,512]{2,1,0:T(8,128)(2,1)} %get-tuple-element.21), channel_id=1, source_target_pairs={{0,2},{2,4},{4,6},{6,8},{8,10},{10,12},{12,14},{14,16},{16,18},{18... | collective-permute-start | bytes 2224136 | tf_op jit(solution)/shard_map/ppermute | solution.py:18
  26.0 26.5 %collective-permute-start.3 = (bf16[1,724,512]{2,1,0:T(8,128)(2,1)}, bf16[1,724,512]{2,1,0:T(8,128)(2,1)}, u32[]{:S(2)}, u32[]{:S(2)}) collective-permute-start(bf16[1,724,512]{2,1,0:T(8,128)(2,1)} %get-tuple-element.22), channel_id=1, source_target_pairs={{2,0},{4,2},{6,4},{8,6},{10,8},{12,10},{14,12},{16,14},{18,16},{20... | collective-permute-start | bytes 2224136 | tf_op jit(solution)/shard_map/ppermute | solution.py:19
  155.2 2.1 copy-start.7
  157.3 54.9 %copy-start.6 = (f32[6]{0:T(128)S(1)}, f32[6]{0:T(128)}, u32[]{:S(2)}) copy-start(f32[6]{0:T(128)} %param.11) | copy-start | bytes 76
  217.2 46.0 %copy-start.3 = (bf16[2,512,512]{2,1,0:T(8,128)(2,1)S(1)}, bf16[2,512,512]{2,1,0:T(8,128)(2,1)}, u32[]{:S(2)}) copy-start(bf16[2,512,512]{2,1,0:T(8,128)(2,1)} %param.12) | copy-start | bytes 3145732
  217.2 37.3 %all-to-all-start = ((bf16[6,512,256]{2,0,1:T(8,128)(2,1)}), bf16[6,512,256]{2,0,1:T(8,128)(2,1)}, u32[]{:S(2)}, u32[]{:S(2)}) async-start(bf16[6,512,256]{2,0,1:T(8,128)(2,1)} %copy.120), calls=%async_computation.1 | async-start | bytes 4194304 | tf_op jit(solution)/shard_map/all_to_all | solution.py:82
  225.6 72.8 %all-gather.3.cloned.1.call-start = ((), (), s32[]{:S(2)}) async-start(), calls=%async_computation.4 | async-start | bytes 3145728 | tf_op jit(solution)/shard_map/all_gather | solution.py:88
  257.6 7.2 %copy-start.5 = (f32[256,512]{1,0:T(8,128)S(1)}, f32[256,512]{1,0:T(8,128)}, u32[]{:S(2)}) copy-start(f32[256,512]{1,0:T(8,128)} %param.13) | copy-start | bytes 1572868
  263.2 123.5 %all-gather.5.cloned.1.call-start = ((), (), s32[]{:S(2)}) async-start(), calls=%async_computation.5 | async-start | bytes 4718592 | tf_op jit(solution)/shard_map/all_gather | solution.py:104
  340.6 54.4 %copy-start.1 = (bf16[1536,512]{1,0:T(8,128)(2,1)S(1)}, bf16[1536,512]{1,0:T(8,128)(2,1)}, u32[]{:S(2)}) copy-start(bf16[1536,512]{1,0:T(8,128)(2,1)} %param.9) | copy-start | bytes 4718596
Sparse Core Ops, SparseCore 0:
  161.7 50.5 reduce-scatter.1
  263.3 35.0 all-gather.2
  340.7 45.8 all-gather.4
where the time goes:
time: 402 us; the launch traced here: 401 us
  waiting for transfers between devices  159 us (40%)
  other arithmetic  88.3 us (22%)
  matrix products  66 us (16%)
  blocking collectives  31.4 us (8%)
  local copies, waits for them, and re-layouts  24.5 us (6%)
  starting transfers between devices  18.8 us (5%)
  between operations  13.4 us (3%)
    convert_element_type x3, other arithmetic, body(): summed = summed + disco_taps[:, :, row_shift, col_shift][:, :, None, None...  67.9 us
    reduce_scatter x1, waiting for transfers between devices, body(): lax.psum_scatter(partial_terms.astype(jnp.bfloat16), 'lon', scatter_dimen...  50.7 us
    dot_general x1, matrix products, body(): jnp.einsum('kijc,kco->ijo', basis_terms, conv_weight, preferred_element_t...  46.6 us
    all_gather x1, waiting for transfers between devices, body(): lax.all_gather(cycle_data, 'lon', axis=2, tiled=True)  46 us
    all_gather x1, waiting for transfers between devices, body(): gathered = lax.all_gather(coeffs, 'lon', axis=3, tiled=True)  33.6 us
    all_to_all x1, blocking collectives, body(): lax.all_to_all(synth, 'lat', split_axis=0, concat_axis=1, tiled=True)  31.4 us
    all_to_all x1, waiting for transfers between devices, body(): lax.all_to_all(weighted, 'lat', split_axis=1, concat_axis=0, tiled=True)  28.8 us
    concatenate x1, other arithmetic, padded_2(): x = jnp.concatenate([before, x, after], axis=dim)  11.9 us
  transfers between devices with their start and end apart: 8, of which 4 were waited for; matrix products, arithmetic and copies ran while one was open for 8% of the time, Pallas kernels for 0%

commit v1 on v0

v1 whole, which is shorter than its diff:
```python
import functools
import math

import jax
import jax.numpy as jnp
import numpy as np
from jax import lax
from jax.experimental import pallas as pl
from jax.experimental.pallas import tpu as pltpu
from jax.sharding import PartitionSpec as P

MESH = pl.DeviceIdType.MESH
C = 512
NLON = 1440
MODES = 256
DEGREES = 256
KERNELS = 3
CYCLES = 6
LATS = 64
LONS = 2
DEVS = LATS * LONS
HALF = NLON // LONS
EDGE = 16
WIDE = HALF + 2 * EDGE
TILE = 48
WINDOW = TILE + 2 * EDGE
PAIRS = ((1, 2), (3, 4), (0, 5))
F32, BF16 = jnp.float32, jnp.bfloat16


def dft_constants():
    j = np.arange(NLON, dtype=np.int64)[:, None]
    m = np.arange(MODES, dtype=np.int64)[None, :]
    angle = ((j * m) % NLON).astype(np.float64) * (2.0 * math.pi / NLON)
    pair = np.stack([np.cos(angle), -np.sin(angle)], axis=2) / math.sqrt(NLON)
    table = pair.reshape(LONS, HALF, 2 * MODES).astype(np.float32)
    forward = np.ascontiguousarray(table.transpose(0, 2, 1))
    return jnp.asarray(forward, BF16), jnp.asarray(table, BF16)


def dot(a, b):
    return jnp.dot(a, b, preferred_element_type=F32)


def build_taps(i, taps, band):
    rows = lax.broadcasted_iota(jnp.int32, (TILE, 3 * WINDOW), 0)
    cols = lax.broadcasted_iota(jnp.int32, (TILE, 3 * WINDOW), 1)
    shift = cols - rows
    for k in range(KERNELS):
        total = jnp.zeros((TILE, 3 * WINDOW), F32)
        for a in range(3):
            for b in range(5):
                value = taps[((k * CYCLES + i) * 3 + a) * 5 + b]
                total = jnp.where(shift == a * WINDOW + EDGE - 2 + b, value, total)
        band[k * TILE : (k + 1) * TILE, :] = total.astype(BF16)


def conv_cycle(i, taps, padded, band, terms, mix, conv):
    build_taps(i, taps, band)

    @pl.loop(0, HALF // TILE)
    def _(t):
        start = pl.multiple_of(t * TILE, 16)
        window = padded[pl.ds(i, 3), pl.ds(start, WINDOW), :].reshape(3 * WINDOW, C)
        basis = dot(band[...], window).astype(BF16)
        for k in range(KERNELS):
            terms[pl.ds(start, TILE), k * C : (k + 1) * C] = basis[k * TILE : (k + 1) * TILE]

    @pl.loop(0, 3)
    def _(t):
        rows = pl.ds(pl.multiple_of(t * 240, 16), 240)
        conv[i, rows, :] = dot(terms[rows, :], mix[...]).astype(BF16)


def dft_pair(p, cycles, quad, forward, conv, spectra, send):
    for s in range(2):

        @pl.loop(0, 2)
        def _(t):
            rows = pl.ds(pl.multiple_of(t * 256, 16), 256)
            spectra[s, rows, :] = dot(forward[rows, :], conv[cycles[s]]) * quad[cycles[s]]

    @pl.loop(0, 8)
    def _(t):
        rows = pl.ds(pl.multiple_of(t * 64, 16), 64)
        first = spectra[0, rows, :].reshape(8, 8, C)
        second = spectra[1, rows, :].reshape(8, 8, C)
        low = lax.broadcasted_iota(jnp.int32, (8, 8, C), 1) < 4
        even = jnp.where(low, first, pltpu.roll(second, 4, 1))
        odd = jnp.where(low, pltpu.roll(first, 4, 1), second)
        both = jnp.stack([even, odd], axis=1).reshape(16, 8, C)
        send[pl.ds(t * 16, 16), p] = both.astype(BF16)


def spread(p, columns_first):
    shape = (LATS * CYCLES, LATS * 8)
    cycle = lax.broadcasted_iota(jnp.int32, shape, 0)
    col = lax.broadcasted_iota(jnp.int32, shape, 1)
    place = (col // 4) % 2
    within = jnp.where(place == 0, PAIRS[p][0], PAIRS[p][1])
    return jnp.where(cycle == (col // 8) * CYCLES + within, 1.0, 0.0).astype(BF16)


def build_triangle(first_order, legendre, ones, table, turned):
    degree = lax.broadcasted_iota(jnp.int32, (DEGREES, LATS * CYCLES), 0)
    for m in range(2):
        values = legendre[m]
        legendre[m] = jnp.where(degree >= first_order + m, values.astype(F32), 0.0).astype(BF16)
    for p in range(3):
        ones[...] = spread(p, False)
        for m in range(2):
            wide = dot(legendre[m], ones[...])
            col = lax.broadcasted_iota(jnp.int32, wide.shape, 1) % 4
            tall = lax.dot_general(
                ones[...], legendre[m], (((0,), (1,)), ((), ())), preferred_element_type=F32
            )
            row = lax.broadcasted_iota(jnp.int32, tall.shape, 0) % 4
            for c in range(2):
                block = slice((2 * m + c) * DEGREES, (2 * m + c + 1) * DEGREES)
                table[p, block, :] = jnp.where(col == 2 * m + c, wide, 0.0).astype(BF16)
                turned[p, :, block] = jnp.where(row == 2 * m + c, tall, 0.0).astype(BF16)


def legendre_pair(p, received, joined, table, coeffs):
    @pl.loop(0, 8)
    def _(t):
        block = received[pl.ds(t * 16, 16), p].astype(F32).reshape(8, 2, 8, C)
        total = (block[:, 0] + block[:, 1]).reshape(64, C)
        joined[pl.ds(pl.multiple_of(t * 64, 16), 64), :] = total.astype(BF16)

    @pl.loop(0, 4)
    def _(t):
        rows = pl.ds(pl.multiple_of(t * 256, 16), 256)
        value = dot(table[p, rows, :], joined[...])
        if p == 0:
            coeffs[rows, :] = value
        else:
            coeffs[rows, :] += value


def mix_modes(coeffs, weight, gain, mixed):
    for m in range(2):
        real = coeffs[2 * m * DEGREES : (2 * m + 1) * DEGREES, :].astype(BF16)
        imag = coeffs[(2 * m + 1) * DEGREES : (2 * m + 2) * DEGREES, :].astype(BF16)
        new_real = (dot(real, weight[0]) - dot(imag, weight[1])) * gain[...]
        mixed[2 * m * DEGREES : (2 * m + 1) * DEGREES, :] = new_real.astype(BF16)
        new_imag = (dot(real, weight[1]) + dot(imag, weight[0])) * gain[...]
        mixed[(2 * m + 1) * DEGREES : (2 * m + 2) * DEGREES, :] = new_imag.astype(BF16)


def synth_pair(p, turned, mixed, send):
    @pl.loop(0, 4)
    def _(t):
        rows = pl.ds(pl.multiple_of(t * 128, 16), 128)
        value = dot(turned[p, rows, :], mixed[...]).astype(BF16).reshape(16, 8, C)
        send[pl.ds(t * 16, 16), p] = value


def inverse_pair(p, cycles, inverse, received, synth, conv, out):
    @pl.loop(0, 8)
    def _(t):
        block = received[pl.ds(t * 16, 16), p].astype(F32).reshape(8, 2, 8, C)
        first, second = block[:, 0], block[:, 1]
        low = lax.broadcasted_iota(jnp.int32, (8, 8, C), 1) < 4
        rows = pl.ds(pl.multiple_of(t * 64, 16), 64)
        even = jnp.where(low, first, pltpu.roll(second, 4, 1))
        odd = jnp.where(low, pltpu.roll(first, 4, 1), second)
        synth[0, rows, :] = even.reshape(64, C).astype(BF16)
        synth[1, rows, :] = odd.reshape(64, C).astype(BF16)

    for s in range(2):

        @pl.loop(0, 3)
        def _(t):
            rows = pl.ds(pl.multiple_of(t * 240, 16), 240)
            value = dot(inverse[rows, :], synth[s]) + conv[cycles[s], rows, :].astype(F32)
            out[cycles[s], rows, :] = value.astype(BF16)


def halo_copies(field, padded, send_sems, recv_sems):
    lat, lon = lax.axis_index("lat"), lax.axis_index("lon")
    up, down, other = (lat + LATS - 1) % LATS, (lat + 1) % LATS, 1 - lon
    head, body, tail = pl.ds(0, EDGE), pl.ds(EDGE, HALF), pl.ds(EDGE + HALF, EDGE)
    last = pl.ds(HALF - EDGE, EDGE)
    inner = pl.ds(1, CYCLES)
    plan = (
        (field.at[:, last], padded.at[inner, head], (lat, other)),
        (field.at[:, head], padded.at[inner, tail], (lat, other)),
        (field.at[0], padded.at[CYCLES + 1, body], (up, lon)),
        (field.at[CYCLES - 1], padded.at[0, body], (down, lon)),
        (field.at[0, last], padded.at[CYCLES + 1, head], (up, other)),
        (field.at[0, head], padded.at[CYCLES + 1, tail], (up, other)),
        (field.at[CYCLES - 1, last], padded.at[0, head], (down, other)),
        (field.at[CYCLES - 1, head], padded.at[0, tail], (down, other)),
    )
    return [
        pltpu.make_async_remote_copy(
            src_ref=src,
            dst_ref=dst,
            send_sem=send_sems.at[n],
            recv_sem=recv_sems.at[n],
            device_id=target,
            device_id_type=MESH,
        )
        for n, (src, dst, target) in enumerate(plan)
    ]


def forward_kernel(
    taps, quad, field, mix, forward_all, conv, send,
    padded, band, terms, forward, spectra, local_sems, send_sems, recv_sems,
):
    lat, lon = lax.axis_index("lat"), lax.axis_index("lon")
    load = pltpu.make_async_copy(field, padded.at[pl.ds(1, CYCLES), pl.ds(EDGE, HALF)], local_sems.at[0])
    load.start()
    table = pltpu.make_async_copy(forward_all.at[lon], forward, local_sems.at[1])
    table.start()
    barrier = pltpu.get_barrier_semaphore()
    up, down = (lat + LATS - 1) % LATS, (lat + 1) % LATS
    for peer in ((lat, 1 - lon), (up, lon), (down, lon), (up, 1 - lon), (down, 1 - lon)):
        pl.semaphore_signal(barrier, inc=1, device_id=peer, device_id_type=MESH)
    pl.semaphore_wait(barrier, 5)
    copies = halo_copies(field, padded, send_sems, recv_sems)
    for copy in copies:
        copy.start()
    load.wait()
    copies[0].wait_recv()
    copies[1].wait_recv()
    table.wait()
    for p, cycles in enumerate(PAIRS):
        if p == 2:
            for copy in copies[2:]:
                copy.wait_recv()

            @pl.when(lat == 0)
            def _():
                padded[0] = jnp.zeros((WIDE, C), BF16)

            @pl.when(lat == LATS - 1)
            def _():
                padded[CYCLES + 1] = jnp.zeros((WIDE, C), BF16)

        for i in cycles:
            conv_cycle(i, taps, padded, band, terms, mix, conv)
        dft_pair(p, cycles, quad, forward, conv, spectra, send)
    for copy in copies:
        copy.wait_send()


def middle_kernel(
    received, legendre_all, weight, gain, send, legendre, ones, table, turned, joined, coeffs, mixed, sems
):
    lat, lon = lax.axis_index("lat"), lax.axis_index("lon")
    load = pltpu.make_async_copy(legendre_all.at[pl.ds(2 * lon, 2)], legendre, sems.at[0])
    load.start()
    load.wait()
    build_triangle(4 * lat + 2 * lon, legendre, ones, table, turned)
    for p in range(3):
        legendre_pair(p, received, joined, table, coeffs)
    mix_modes(coeffs, weight, gain, mixed)
    for p in range(3):
        synth_pair(p, turned, mixed, send)


def inverse_kernel(received, conv, inverse_all, out, inverse, synth, sems):
    lon = lax.axis_index("lon")
    load = pltpu.make_async_copy(inverse_all.at[lon], inverse, sems.at[0])
    load.start()
    load.wait()
    for p, cycles in enumerate(PAIRS):
        inverse_pair(p, cycles, inverse, received, synth, conv, out)


VMEM = pl.BlockSpec(memory_space=pltpu.VMEM)
SMEM = pl.BlockSpec(memory_space=pltpu.SMEM)
ANY = pl.BlockSpec(memory_space=pl.ANY)
LIMIT = 56 * 2**20


def body(grid_field, disco_taps, disco_mix, legendre, quad_weights, mix_weight, degree_gain):
    forward_all, inverse_all = dft_constants()
    conv, send = pl.pallas_call(
        forward_kernel,
        out_shape=(
            jax.ShapeDtypeStruct((CYCLES, HALF, C), BF16),
            jax.ShapeDtypeStruct((DEVS, 3, 8, C), BF16),
        ),
        in_specs=[SMEM, SMEM, ANY, VMEM, ANY],
        out_specs=(VMEM, VMEM),
        scratch_shapes=[
            pltpu.VMEM((CYCLES + 2, WIDE, C), BF16),
            pltpu.VMEM((KERNELS * TILE, 3 * WINDOW), BF16),
            pltpu.VMEM((HALF, KERNELS * C), BF16),
            pltpu.VMEM((2 * MODES, HALF), BF16),
            pltpu.VMEM((2, 2 * MODES, C), F32),
            pltpu.SemaphoreType.DMA((2,)),
            pltpu.SemaphoreType.DMA((8,)),
            pltpu.SemaphoreType.DMA((8,)),
        ],
        compiler_params=pltpu.CompilerParams(
            collective_id=0, has_side_effects=True, vmem_limit_bytes=LIMIT
        ),
    )(disco_taps.reshape(-1), quad_weights, grid_field, disco_mix, forward_all)
    received = lax.all_to_all(send, ("lat", "lon"), split_axis=0, concat_axis=0, tiled=True)
    synth = pl.pallas_call(
        middle_kernel,
        out_shape=jax.ShapeDtypeStruct((LATS, 3, 8, C), BF16),
        in_specs=[VMEM, ANY, VMEM, VMEM],
        out_specs=VMEM,
        scratch_shapes=[
            pltpu.VMEM((2, DEGREES, LATS * CYCLES), BF16),
            pltpu.VMEM((LATS * CYCLES, LATS * 8), BF16),
            pltpu.VMEM((3, 4 * DEGREES, LATS * 8), BF16),
            pltpu.VMEM((3, LATS * 8, 4 * DEGREES), BF16),
            pltpu.VMEM((LATS * 8, C), BF16),
            pltpu.VMEM((4 * DEGREES, C), F32),
            pltpu.VMEM((4 * DEGREES, C), BF16),
            pltpu.SemaphoreType.DMA((1,)),
        ],
        compiler_params=pltpu.CompilerParams(vmem_limit_bytes=LIMIT),
    )(received, legendre, mix_weight, degree_gain)
    doubled = jnp.broadcast_to(synth[:, None], (LATS, 2, 3, 8, C)).reshape(DEVS, 3, 8, C)
    returned = lax.all_to_all(doubled, ("lat", "lon"), split_axis=0, concat_axis=0, tiled=True)
    return pl.pallas_call(
        inverse_kernel,
        out_shape=jax.ShapeDtypeStruct((CYCLES, HALF, C), BF16),
        in_specs=[VMEM, VMEM, ANY],
        out_specs=VMEM,
        scratch_shapes=[
            pltpu.VMEM((HALF, 2 * MODES), BF16),
            pltpu.VMEM((2, 2 * MODES, C), BF16),
            pltpu.SemaphoreType.DMA((1,)),
        ],
        compiler_params=pltpu.CompilerParams(vmem_limit_bytes=LIMIT),
    )(returned, conv, inverse_all)


def solution(mesh):
    return jax.shard_map(
        body,
        mesh=mesh,
        in_specs=(
            P("lat", "lon", None),
            P(None, "lat", None, None),
            P(),
            P("lat", None, None),
            P("lat"),
            P(),
            P(),
        ),
        out_specs=P("lat", "lon", None),
        check_vma=False,
    )
```

time: 402 us -> 186 us (0.46)
  waiting for transfers between devices: 159 us -> 0 us
  other arithmetic: 88.3 us -> 0 us
  blocking collectives: 31.4 us -> 108 us
  Pallas kernels: 0 us -> 74.7 us
  matrix products: 66 us -> 0 us
  local copies, waits for them, and re-layouts: 24.5 us -> 3.29 us
  starting transfers between devices: 18.8 us -> 0 us
  between operations: 13.4 us -> 0.03 us
    all_gather x2 -> x0, waiting for transfers between devices: 79.6 us -> none  [the longest x1 46 us: body(): lax.all_gather(cycle_data, 'lon', axis=2, tiled=True)]
    all_to_all x1 -> x2, blocking collectives: 31.4 us -> 108 us  [the longest x1 61.6 us: body(): lax.all_to_all(send, ('lat', 'lon'), split_axis=0, concat_axis=0, tiled=T...]
    pallas_call x0 -> x3, Pallas kernels: none -> 74.7 us  [the longest x1 46.3 us: body(): pl.pallas_call(forward_kernel, out_shape=(jax.ShapeDtypeStruct((CYCLES, H...]
    convert_element_type x5 -> x0, other arithmetic: 70 us -> none  [the longest x3 67.9 us: body(): summed = summed + disco_taps[:, :, row_shift, col_shift][:, :, None, None...]
    dot_general x5 -> x0, matrix products: 66 us -> none  [the longest x1 46.6 us: body(): jnp.einsum('kijc,kco->ijo', basis_terms, conv_weight, preferred_element_t...]
    reduce_scatter x1 -> x0, waiting for transfers between devices: 50.7 us -> none  [body(): lax.psum_scatter(partial_terms.astype(jnp.bfloat16), 'lon', scatter_dimen...]
    all_to_all x1 -> x0, waiting for transfers between devices: 28.8 us -> none  [body(): lax.all_to_all(weighted, 'lat', split_axis=1, concat_axis=0, tiled=True)]
    concatenate x1 -> x0, other arithmetic: 11.9 us -> none  [padded_2(): x = jnp.concatenate([before, x, after], axis=dim)]
  transfers between devices with their start and end apart: 8 -> 0, of which waited for: 4 -> 0; matrix products, arithmetic and copies ran while one was open for 8% -> 0% of each run, Pallas kernels for 0% -> 0%
where the time goes in v1:
time: 186 us
  blocking collectives  108 us (58%)
  Pallas kernels  74.7 us (40%)
  local copies, waits for them, and re-layouts  3.29 us (2%)
    all_to_all x1, blocking collectives, body(): lax.all_to_all(send, ('lat', 'lon'), split_axis=0, concat_axis=0, tiled=T...  61.6 us
    all_to_all x1, blocking collectives, body(): lax.all_to_all(doubled, ('lat', 'lon'), split_axis=0, concat_axis=0, tile...  46.3 us
    pallas_call x1, Pallas kernels, body(): pl.pallas_call(forward_kernel, out_shape=(jax.ShapeDtypeStruct((CYCLES, H...  46.3 us
    pallas_call x1, Pallas kernels, body(): pl.pallas_call(middle_kernel, out_shape=jax.ShapeDtypeStruct((LATS, 3, 8,...  15.7 us
    pallas_call x1, Pallas kernels, body(): pl.pallas_call(inverse_kernel, out_shape=jax.ShapeDtypeStruct((CYCLES, HA...  12.7 us

profile of v1, /device:TPU:1, one launch (start us, length us, event | category | flops | bytes accessed | tf_op | source)
XLA Modules:
  0.0 185.9 jit_solution(17166330147606042429)
XLA Ops:
  0.0 0.9 copy.10
  0.9 0.7 reshape.7.taps
  1.6 46.3 %shard_map.91 = (bf16[6,720,512]{2,1,0:T(8,128)(2,1)}, bf16[128,3,8,512]{3,2,1,0:T(8,128)(2,1)}) custom-call(f32[270]{0:T(512)} %reshape.7.taps, f32[6]{0:T(128)} %quad.1, bf16[6,720,512]{2,1,0:T(8,128)(2,1)} %field.1, bf16[1536,512]{1,0:T(8,128)(2,1)} %mix.1, bf16[2,512,720]{2,1,0:T(8,128)(2,1)} %constant.4.clone.forward_all), custom_call_target="tpu_custom_call" | custom-call | tf_op jit(solution)/shard_map/pallas_call | solution.py:282
  47.9 61.6 %all_to_all.10.received = bf16[128,3,8,512]{3,2,1,0:T(8,128)(2,1)} all-to-all(bf16[128,3,8,512]{3,2,1,0:T(8,128)(2,1)} %get-tuple-element.7), channel_id=1, replica_groups=mesh['lat'=64,'lon'=2] {'lat','lon'}, dimensions={0} | all-to-all | bytes 6291456 | tf_op jit(solution)/shard_map/all_to_all | solution.py:304
  109.5 15.7 %shard_map.92 = bf16[64,3,8,512]{3,2,1,0:T(8,128)(2,1)} custom-call(bf16[128,3,8,512]{3,2,1,0:T(8,128)(2,1)} %all_to_all.10.received, bf16[4,256,384]{2,1,0:T(8,128)(2,1)} %legendre_all.1, bf16[2,512,512]{2,1,0:T(8,128)(2,1)} %weight.1, f32[256,512]{1,0:T(8,128)} %gain.1), custom_call_target="tpu_custom_call" | custom-call | tf_op jit(solution)/shard_map/pallas_call | solution.py:305
  125.2 1.7 broadcast_in_dim.2
  126.9 46.3 %all_to_all.11.received = bf16[128,3,8,512]{3,2,1,0:T(8,128)(2,1)} all-to-all(bf16[128,3,8,512]{3,2,1,0:T(8,128)(2,1)S(1)} %bitcast.1), channel_id=1, replica_groups=mesh['lat'=64,'lon'=2] {'lat','lon'}, dimensions={0} | all-to-all | bytes 6291456 | tf_op jit(solution)/shard_map/all_to_all | solution.py:323
  173.2 12.7 %shard_map.93 = bf16[6,720,512]{2,1,0:T(8,128)(2,1)} custom-call(bf16[128,3,8,512]{3,2,1,0:T(8,128)(2,1)} %all_to_all.11.received, bf16[6,720,512]{2,1,0:T(8,128)(2,1)} %get-tuple-element.8.conv, bf16[2,720,512]{2,1,0:T(8,128)(2,1)} %constant.5.clone.inverse_all), custom_call_target="tpu_custom_call" | custom-call | tf_op jit(solution)/shard_map/pallas_call | solution.py:324

commit v2 on v1

--- a/solution.py
+++ b/solution.py
@@ -1,4 +1,3 @@
-import functools
 import math
 
 import jax
@@ -19,6 +18,8 @@
 LATS = 64
 LONS = 2
 DEVS = LATS * LONS
+CHIPS = 64
+STRIDE = 43
 HALF = NLON // LONS
 EDGE = 16
 WIDE = HALF + 2 * EDGE
@@ -55,17 +56,26 @@
         band[k * TILE : (k + 1) * TILE, :] = total.astype(BF16)
 
 
-def conv_cycle(i, taps, padded, band, terms, mix, conv):
-    build_taps(i, taps, band)
-
-    @pl.loop(0, HALF // TILE)
-    def _(t):
-        start = pl.multiple_of(t * TILE, 16)
-        window = padded[pl.ds(i, 3), pl.ds(start, WINDOW), :].reshape(3 * WINDOW, C)
-        basis = dot(band[...], window).astype(BF16)
-        for k in range(KERNELS):
-            terms[pl.ds(start, TILE), k * C : (k + 1) * C] = basis[k * TILE : (k + 1) * TILE]
-
+def basis_tile(i, t, padded, band, terms):
+    start = pl.multiple_of(t * TILE, 16)
+    window = padded[pl.ds(i, 3), pl.ds(start, WINDOW), :].reshape(3 * WINDOW, C)
+    basis = dot(band[...], window).astype(BF16)
+    for k in range(KERNELS):
+        terms[pl.ds(start, TILE), k * C : (k + 1) * C] = basis[k * TILE : (k + 1) * TILE]
+
+
+def basis_inner(i, padded, band, terms):
+    @pl.loop(1, HALF // TILE - 1)
+    def _(t):
+        basis_tile(i, t, padded, band, terms)
+
+
+def basis_edges(i, padded, band, terms):
+    basis_tile(i, 0, padded, band, terms)
+    basis_tile(i, HALF // TILE - 1, padded, band, terms)
+
+
+def mix_terms(i, terms, mix, conv):
     @pl.loop(0, 3)
     def _(t):
         rows = pl.ds(pl.multiple_of(t * 240, 16), 240)
@@ -89,7 +99,7 @@
         even = jnp.where(low, first, pltpu.roll(second, 4, 1))
         odd = jnp.where(low, pltpu.roll(first, 4, 1), second)
         both = jnp.stack([even, odd], axis=1).reshape(16, 8, C)
-        send[pl.ds(t * 16, 16), p] = both.astype(BF16)
+        send[p, pl.ds(t * 16, 16)] = both.astype(BF16)
 
 
 def spread(p, columns_first):
@@ -124,7 +134,7 @@
 def legendre_pair(p, received, joined, table, coeffs):
     @pl.loop(0, 8)
     def _(t):
-        block = received[pl.ds(t * 16, 16), p].astype(F32).reshape(8, 2, 8, C)
+        block = received[p, pl.ds(t * 16, 16)].astype(F32).reshape(8, 2, 8, C)
         total = (block[:, 0] + block[:, 1]).reshape(64, C)
         joined[pl.ds(pl.multiple_of(t * 64, 16), 64), :] = total.astype(BF16)
 
@@ -153,13 +163,13 @@
     def _(t):
         rows = pl.ds(pl.multiple_of(t * 128, 16), 128)
         value = dot(turned[p, rows, :], mixed[...]).astype(BF16).reshape(16, 8, C)
-        send[pl.ds(t * 16, 16), p] = value
+        send[p, pl.ds(t * 16, 16)] = value
 
 
 def inverse_pair(p, cycles, inverse, received, synth, conv, out):
     @pl.loop(0, 8)
     def _(t):
-        block = received[pl.ds(t * 16, 16), p].astype(F32).reshape(8, 2, 8, C)
+        block = received[p, pl.ds(t * 16, 16)].astype(F32).reshape(8, 2, 8, C)
         first, second = block[:, 0], block[:, 1]
         low = lax.broadcasted_iota(jnp.int32, (8, 8, C), 1) < 4
         rows = pl.ds(pl.multiple_of(t * 64, 16), 64)
@@ -206,27 +216,88 @@
     ]
 
 
-def forward_kernel(
-    taps, quad, field, mix, forward_all, conv, send,
-    padded, band, terms, forward, spectra, local_sems, send_sems, recv_sems,
+def partner(s, core):
+    lat, lon = lax.axis_index("lat"), lax.axis_index("lon")
+    x, z, y = lat // 16, (lat // 4) % 4, (lat // 2) % 2 + 2 * lon
+    x, z, y = (x + s // 16) % 4, (z + (s // 4) % 4) % 4, (y + s % 4) % 4
+    return ((x * 4 + z) * 2 + y % 2) * 2 + (lat + core) % 2, y // 2
+
+
+def for_partners(act):
+    act(*partner(0, 1))
+
+    def step(s, carry):
+        far = (s * STRIDE) % CHIPS
+        act(*partner(far, 0))
+        act(*partner(far, 1))
+        return carry
+
+    lax.fori_loop(1, CHIPS, step, 0)
+
+
+def scatter(p, pick, received, send_sem, recv_sem):
+    me = lax.axis_index("lat") * LONS + lax.axis_index("lon")
+
+    def act(lat, lon):
+        pltpu.make_async_remote_copy(
+            src_ref=pick(lat, lon),
+            dst_ref=received.at[p, me],
+            send_sem=send_sem,
+            recv_sem=recv_sem,
+            device_id=(lat, lon),
+            device_id_type=MESH,
+        ).start()
+
+    for_partners(act)
+
+
+def arrival(p, received, send_sem, recv_sem):
+    return pltpu.make_async_remote_copy(
+        src_ref=received.at[p, pl.ds(0, DEVS - 1)],
+        dst_ref=received.at[p, pl.ds(0, DEVS - 1)],
+        send_sem=send_sem,
+        recv_sem=recv_sem,
+        device_id=partner(0, 1),
+        device_id_type=MESH,
+    )
+
+
+def kernel(
+    taps, quad, field, mix, forward_all, inverse_all, legendre_all, weight, gain, out,
+    padded, band, terms, forward, spectra, conv, send, received,
+    legendre, ones, table, turned, joined, coeffs, mixed, back, returned, inverse, synth,
+    local_sems, halo_send, halo_recv, go_send, go_recv, back_send, back_recv,
 ):
     lat, lon = lax.axis_index("lat"), lax.axis_index("lon")
-    load = pltpu.make_async_copy(field, padded.at[pl.ds(1, CYCLES), pl.ds(EDGE, HALF)], local_sems.at[0])
-    load.start()
-    table = pltpu.make_async_copy(forward_all.at[lon], forward, local_sems.at[1])
-    table.start()
+    me = lat * LONS + lon
+    loads = [
+        pltpu.make_async_copy(src, dst, local_sems.at[n])
+        for n, (src, dst) in enumerate(
+            (
+                (field, padded.at[pl.ds(1, CYCLES), pl.ds(EDGE, HALF)]),
+                (forward_all.at[lon], forward),
+                (inverse_all.at[lon], inverse),
+                (legendre_all.at[pl.ds(2 * lon, 2)], legendre),
+            )
+        )
+    ]
+    for load in loads:
+        load.start()
     barrier = pltpu.get_barrier_semaphore()
-    up, down = (lat + LATS - 1) % LATS, (lat + 1) % LATS
-    for peer in ((lat, 1 - lon), (up, lon), (down, lon), (up, 1 - lon), (down, 1 - lon)):
-        pl.semaphore_signal(barrier, inc=1, device_id=peer, device_id_type=MESH)
-    pl.semaphore_wait(barrier, 5)
-    copies = halo_copies(field, padded, send_sems, recv_sems)
+
+    def greet(a, b):
+        pl.semaphore_signal(barrier, inc=1, device_id=(a, b), device_id_type=MESH)
+
+    for_partners(greet)
+    loads[0].wait()
+    build_taps(1, taps, band)
+    basis_inner(1, padded, band, terms.at[0])
+    pl.semaphore_wait(barrier, DEVS - 1)
+    copies = halo_copies(field, padded, halo_send, halo_recv)
     for copy in copies:
         copy.start()
-    load.wait()
-    copies[0].wait_recv()
-    copies[1].wait_recv()
-    table.wait()
+    for load in loads[1:]:
+        load.wait()
     for p, cycles in enumerate(PAIRS):
         if p == 2:
             for copy in copies[2:]:
@@ -240,74 +311,65 @@
             def _():
                 padded[CYCLES + 1] = jnp.zeros((WIDE, C), BF16)
 
-        for i in cycles:
-            conv_cycle(i, taps, padded, band, terms, mix, conv)
+        if p > 0:
+            build_taps(cycles[0], taps, band)
+            basis_inner(cycles[0], padded, band, terms.at[0])
+        else:
+            copies[0].wait_recv()
+            copies[1].wait_recv()
+        basis_edges(cycles[0], padded, band, terms.at[0])
+        mix_terms(cycles[0], terms.at[0], mix, conv)
+        build_taps(cycles[1], taps, band)
+        basis_inner(cycles[1], padded, band, terms.at[1])
+        basis_edges(cycles[1], padded, band, terms.at[1])
+        mix_terms(cycles[1], terms.at[1], mix, conv)
         dft_pair(p, cycles, quad, forward, conv, spectra, send)
-    for copy in copies:
-        copy.wait_send()
-
-
-def middle_kernel(
-    received, legendre_all, weight, gain, send, legendre, ones, table, turned, joined, coeffs, mixed, sems
-):
-    lat, lon = lax.axis_index("lat"), lax.axis_index("lon")
-    load = pltpu.make_async_copy(legendre_all.at[pl.ds(2 * lon, 2)], legendre, sems.at[0])
-    load.start()
-    load.wait()
+        scatter(
+            p, lambda a, b: send.at[p, a * LONS + b], received, go_send.at[p], go_recv.at[p]
+        )
+        received[p, me] = send[p, me]
     build_triangle(4 * lat + 2 * lon, legendre, ones, table, turned)
     for p in range(3):
+        arrival(p, received, go_send.at[p], go_recv.at[p]).wait_recv()
         legendre_pair(p, received, joined, table, coeffs)
     mix_modes(coeffs, weight, gain, mixed)
     for p in range(3):
-        synth_pair(p, turned, mixed, send)
-
-
-def inverse_kernel(received, conv, inverse_all, out, inverse, synth, sems):
-    lon = lax.axis_index("lon")
-    load = pltpu.make_async_copy(inverse_all.at[lon], inverse, sems.at[0])
-    load.start()
-    load.wait()
+        synth_pair(p, turned, mixed, back)
+        scatter(p, lambda a, b: back.at[p, a], returned, back_send.at[p], back_recv.at[p])
+        returned[p, me] = back[p, lat]
     for p, cycles in enumerate(PAIRS):
-        inverse_pair(p, cycles, inverse, received, synth, conv, out)
+        arrival(p, returned, back_send.at[p], back_recv.at[p]).wait_recv()
+        inverse_pair(p, cycles, inverse, returned, synth, conv, out)
+    for copy in copies:
+        copy.wait_send()
+    for p in range(3):
+        arrival(p, received, go_send.at[p], go_recv.at[p]).wait_send()
+        arrival(p, returned, back_send.at[p], back_recv.at[p]).wait_send()
 
 
 VMEM = pl.BlockSpec(memory_space=pltpu.VMEM)
 SMEM = pl.BlockSpec(memory_space=pltpu.SMEM)
 ANY = pl.BlockSpec(memory_space=pl.ANY)
-LIMIT = 56 * 2**20
+LIMIT = 60 * 2**20
 
 
 def body(grid_field, disco_taps, disco_mix, legendre, quad_weights, mix_weight, degree_gain):
     forward_all, inverse_all = dft_constants()
-    conv, send = pl.pallas_call(
-        forward_kernel,
-        out_shape=(
-            jax.ShapeDtypeStruct((CYCLES, HALF, C), BF16),
-            jax.ShapeDtypeStruct((DEVS, 3, 8, C), BF16),
-        ),
-        in_specs=[SMEM, SMEM, ANY, VMEM, ANY],
-        out_specs=(VMEM, VMEM),
+    dma = pltpu.SemaphoreType.DMA
+    return pl.pallas_call(
+        kernel,
+        out_shape=jax.ShapeDtypeStruct((CYCLES, HALF, C), BF16),
+        in_specs=[SMEM, SMEM, ANY, VMEM, ANY, ANY, ANY, VMEM, VMEM],
+        out_specs=VMEM,
         scratch_shapes=[
             pltpu.VMEM((CYCLES + 2, WIDE, C), BF16),
             pltpu.VMEM((KERNELS * TILE, 3 * WINDOW), BF16),
-            pltpu.VMEM((HALF, KERNELS * C), BF16),
+            pltpu.VMEM((2, HALF, KERNELS * C), BF16),
             pltpu.VMEM((2 * MODES, HALF), BF16),
             pltpu.VMEM((2, 2 * MODES, C), F32),
-            pltpu.SemaphoreType.DMA((2,)),
-            pltpu.SemaphoreType.DMA((8,)),
-            pltpu.SemaphoreType.DMA((8,)),
-        ],
-        compiler_params=pltpu.CompilerParams(
-            collective_id=0, has_side_effects=True, vmem_limit_bytes=LIMIT
-        ),
-    )(disco_taps.reshape(-1), quad_weights, grid_field, disco_mix, forward_all)
-    received = lax.all_to_all(send, ("lat", "lon"), split_axis=0, concat_axis=0, tiled=True)
-    synth = pl.pallas_call(
-        middle_kernel,
-        out_shape=jax.ShapeDtypeStruct((LATS, 3, 8, C), BF16),
-        in_specs=[VMEM, ANY, VMEM, VMEM],
-        out_specs=VMEM,
-        scratch_shapes=[
+            pltpu.VMEM((CYCLES, HALF, C), BF16),
+            pltpu.VMEM((3, DEVS, 8, C), BF16),
+            pltpu.VMEM((3, DEVS, 8, C), BF16),
             pltpu.VMEM((2, DEGREES, LATS * CYCLES), BF16),
             pltpu.VMEM((LATS * CYCLES, LATS * 8), BF16),
             pltpu.VMEM((3, 4 * DEGREES, LATS * 8), BF16),
@@ -315,24 +377,32 @@
             pltpu.VMEM((LATS * 8, C), BF16),
             pltpu.VMEM((4 * DEGREES, C), F32),
             pltpu.VMEM((4 * DEGREES, C), BF16),
-            pltpu.SemaphoreType.DMA((1,)),
-        ],
-        compiler_params=pltpu.CompilerParams(vmem_limit_bytes=LIMIT),
-    )(received, legendre, mix_weight, degree_gain)
-    doubled = jnp.broadcast_to(synth[:, None], (LATS, 2, 3, 8, C)).reshape(DEVS, 3, 8, C)
-    returned = lax.all_to_all(doubled, ("lat", "lon"), split_axis=0, concat_axis=0, tiled=True)
-    return pl.pallas_call(
-        inverse_kernel,
-        out_shape=jax.ShapeDtypeStruct((CYCLES, HALF, C), BF16),
-        in_specs=[VMEM, VMEM, ANY],
-        out_specs=VMEM,
-        scratch_shapes=[
+            pltpu.VMEM((3, LATS, 8, C), BF16),
+            pltpu.VMEM((3, DEVS, 8, C), BF16),
             pltpu.VMEM((HALF, 2 * MODES), BF16),
             pltpu.VMEM((2, 2 * MODES, C), BF16),
-            pltpu.SemaphoreType.DMA((1,)),
+            dma((4,)),
+            dma((8,)),
+            dma((8,)),
+            dma((3,)),
+            dma((3,)),
+            dma((3,)),
+            dma((3,)),
         ],
-        compiler_params=pltpu.CompilerParams(vmem_limit_bytes=LIMIT),
-    )(returned, conv, inverse_all)
+        compiler_params=pltpu.CompilerParams(
+            collective_id=0, has_side_effects=True, vmem_limit_bytes=LIMIT
+        ),
+    )(
+        disco_taps.reshape(-1),
+        quad_weights,
+        grid_field,
+        disco_mix,
+        forward_all,
+        inverse_all,
+        legendre,
+        mix_weight,
+        degree_gain,
+    )
 
 
 def solution(mesh):

time: 186 us -> 134 us (0.72)
  blocking collectives: 108 us -> 0 us
  Pallas kernels: 74.7 us -> 127 us
  local copies, waits for them, and re-layouts: 3.29 us -> 6.34 us
    all_to_all x2 -> x0, blocking collectives: 108 us -> none  [the longest x1 61.6 us: body(): lax.all_to_all(send, ('lat', 'lon'), split_axis=0, concat_axis=0, tiled=T...]
    pallas_call x3 -> x1, Pallas kernels: 74.7 us -> 127 us  [body(): pl.pallas_call(kernel, out_shape=jax.ShapeDtypeStruct((CYCLES, HALF, C),...]
    unnamed x1 -> x2, local copies, waits for them, and re-layouts: 0.9 us -> 5.62 us
where the time goes in v2:
time: 134 us
  Pallas kernels  127 us (95%)
  local copies, waits for them, and re-layouts  6.34 us (5%)
    pallas_call x1, Pallas kernels, body(): pl.pallas_call(kernel, out_shape=jax.ShapeDtypeStruct((CYCLES, HALF, C),...  127 us
    unnamed x2, local copies, waits for them, and re-layouts  5.62 us

profile of v2, /device:TPU:1, one launch (start us, length us, event | category | flops | bytes accessed | tf_op | source)
XLA Modules:
  0.0 133.8 jit_solution(11153906318708352306)
XLA Ops:
  0.0 0.9 copy.10
  0.9 0.7 reshape.3.taps
  1.6 127.5 %shard_map.91 = bf16[6,720,512]{2,1,0:T(8,128)(2,1)} custom-call(f32[270]{0:T(512)} %reshape.3.taps, f32[6]{0:T(128)} %quad.1, bf16[6,720,512]{2,1,0:T(8,128)(2,1)} %field.1, bf16[1536,512]{1,0:T(8,128)(2,1)} %mix.1, bf16[2,512,720]{2,1,0:T(8,128)(2,1)} %constant.4.clone.forward_all, bf16[2,720,512]{2,1,0:T(8,128)(2,1)} %constant.5.clone.inverse_all, ...), custom_call_target="tpu_custom_call" | custom-call | tf_op jit(solution)/shard_map/pallas_call | solution.py:359
  129.1 4.7 %copy.12 = bf16[6,720,512]{2,1,0:T(8,128)(2,1)} copy(bf16[6,720,512]{2,1,0:T(8,128)(2,1)} %shard_map.91) | data formatting | bytes 8847360

commit v3 on v2

--- a/solution.py
+++ b/solution.py
@@ -51,7 +51,7 @@
         total = jnp.zeros((TILE, 3 * WINDOW), F32)
         for a in range(3):
             for b in range(5):
-                value = taps[((k * CYCLES + i) * 3 + a) * 5 + b]
+                value = taps[k, i, a, b]
                 total = jnp.where(shift == a * WINDOW + EDGE - 2 + b, value, total)
         band[k * TILE : (k + 1) * TILE, :] = total.astype(BF16)
 
@@ -65,30 +65,24 @@
 
 
 def basis_inner(i, padded, band, terms):
-    @pl.loop(1, HALF // TILE - 1)
-    def _(t):
+    for t in range(1, HALF // TILE - 1):
         basis_tile(i, t, padded, band, terms)
 
 
 def basis_edges(i, padded, band, terms):
-    basis_tile(i, 0, padded, band, terms)
-    basis_tile(i, HALF // TILE - 1, padded, band, terms)
+    for t in (0, HALF // TILE - 1):
+        basis_tile(i, t, padded, band, terms)
 
 
 def mix_terms(i, terms, mix, conv):
-    @pl.loop(0, 3)
-    def _(t):
-        rows = pl.ds(pl.multiple_of(t * 240, 16), 240)
+    for t in range(3):
+        rows = slice(t * 240, (t + 1) * 240)
         conv[i, rows, :] = dot(terms[rows, :], mix[...]).astype(BF16)
 
 
 def dft_pair(p, cycles, quad, forward, conv, spectra, send):
     for s in range(2):
-
-        @pl.loop(0, 2)
-        def _(t):
-            rows = pl.ds(pl.multiple_of(t * 256, 16), 256)
-            spectra[s, rows, :] = dot(forward[rows, :], conv[cycles[s]]) * quad[cycles[s]]
+        spectra[s] = dot(forward[...], conv[cycles[s]]) * quad[cycles[s]]
 
     @pl.loop(0, 8)
     def _(t):
@@ -138,14 +132,11 @@
         total = (block[:, 0] + block[:, 1]).reshape(64, C)
         joined[pl.ds(pl.multiple_of(t * 64, 16), 64), :] = total.astype(BF16)
 
-    @pl.loop(0, 4)
-    def _(t):
-        rows = pl.ds(pl.multiple_of(t * 256, 16), 256)
-        value = dot(table[p, rows, :], joined[...])
-        if p == 0:
-            coeffs[rows, :] = value
-        else:
-            coeffs[rows, :] += value
+    value = dot(table[p], joined[...])
+    if p == 0:
+        coeffs[...] = value
+    else:
+        coeffs[...] += value
 
 
 def mix_modes(coeffs, weight, gain, mixed):
@@ -159,14 +150,10 @@
 
 
 def synth_pair(p, turned, mixed, send):
-    @pl.loop(0, 4)
-    def _(t):
-        rows = pl.ds(pl.multiple_of(t * 128, 16), 128)
-        value = dot(turned[p, rows, :], mixed[...]).astype(BF16).reshape(16, 8, C)
-        send[p, pl.ds(t * 16, 16)] = value
-
-
-def inverse_pair(p, cycles, inverse, received, synth, conv, out):
+    send[p] = dot(turned[p], mixed[...]).astype(BF16).reshape(LATS, 8, C)
+
+
+def inverse_pair(p, cycles, inverse, received, synth, conv):
     @pl.loop(0, 8)
     def _(t):
         block = received[p, pl.ds(t * 16, 16)].astype(F32).reshape(8, 2, 8, C)
@@ -179,12 +166,8 @@
         synth[1, rows, :] = odd.reshape(64, C).astype(BF16)
 
     for s in range(2):
-
-        @pl.loop(0, 3)
-        def _(t):
-            rows = pl.ds(pl.multiple_of(t * 240, 16), 240)
-            value = dot(inverse[rows, :], synth[s]) + conv[cycles[s], rows, :].astype(F32)
-            out[cycles[s], rows, :] = value.astype(BF16)
+        value = dot(inverse[...], synth[s]) + conv[cycles[s]].astype(F32)
+        conv[cycles[s]] = value.astype(BF16)
 
 
 def halo_copies(field, padded, send_sems, recv_sems):
@@ -218,16 +201,16 @@
 
 def partner(s, core):
     lat, lon = lax.axis_index("lat"), lax.axis_index("lon")
-    x, z, y = lat // 16, (lat // 4) % 4, (lat // 2) % 2 + 2 * lon
-    x, z, y = (x + s // 16) % 4, (z + (s // 4) % 4) % 4, (y + s % 4) % 4
-    return ((x * 4 + z) * 2 + y % 2) * 2 + (lat + core) % 2, y // 2
+    x, z, y = lat >> 4, (lat >> 2) & 3, ((lat >> 1) & 1) + 2 * lon
+    x, z, y = (x + (s >> 4)) & 3, (z + (s >> 2)) & 3, (y + s) & 3
+    return (x << 4) + (z << 2) + ((y & 1) << 1) + ((lat + core) & 1), y >> 1
 
 
 def for_partners(act):
     act(*partner(0, 1))
 
     def step(s, carry):
-        far = (s * STRIDE) % CHIPS
+        far = (s * STRIDE) & (CHIPS - 1)
         act(*partner(far, 0))
         act(*partner(far, 1))
         return carry
@@ -262,40 +245,56 @@
     )
 
 
+def axis_peers():
+    far = [16 * d for d in (1, 2, 3)] + [4 * d for d in (1, 2, 3)] + [1, 2, 3]
+    return [partner(0, 1)] + [partner(d, 0) for d in far]
+
+
+def signal_all(semaphore, peers):
+    for peer in peers:
+        pl.semaphore_signal(semaphore, inc=1, device_id=peer, device_id_type=MESH)
+
+
 def kernel(
-    taps, quad, field, mix, forward_all, inverse_all, legendre_all, weight, gain, out,
-    padded, band, terms, forward, spectra, conv, send, received,
-    legendre, ones, table, turned, joined, coeffs, mixed, back, returned, inverse, synth,
-    local_sems, halo_send, halo_recv, go_send, go_recv, back_send, back_recv,
+    taps, quad, field, mix_all, forward_all, inverse_all, legendre_all, weight_all, gain_all, out,
+    padded, band, terms, mix, forward, spectra, conv, send, received,
+    legendre, ones, table, turned, joined, coeffs, weight, gain, mixed,
+    back, returned, inverse, synth,
+    rounds, local_sems, out_sems, halo_send, halo_recv, go_send, go_recv, back_send, back_recv,
 ):
     lat, lon = lax.axis_index("lat"), lax.axis_index("lon")
     me = lat * LONS + lon
+    up, down, other = (lat + LATS - 1) % LATS, (lat + 1) % LATS, 1 - lon
+    barrier = pltpu.get_barrier_semaphore()
+    near = axis_peers()
+    beside = [(up, lon), (down, lon), (up, other), (down, other)]
+    signal_all(barrier, near + beside)
     loads = [
         pltpu.make_async_copy(src, dst, local_sems.at[n])
         for n, (src, dst) in enumerate(
             (
                 (field, padded.at[pl.ds(1, CYCLES), pl.ds(EDGE, HALF)]),
+                (mix_all, mix),
                 (forward_all.at[lon], forward),
+                (legendre_all.at[pl.ds(2 * lon, 2)], legendre),
+                (weight_all, weight),
+                (gain_all, gain),
                 (inverse_all.at[lon], inverse),
-                (legendre_all.at[pl.ds(2 * lon, 2)], legendre),
             )
         )
     ]
     for load in loads:
         load.start()
-    barrier = pltpu.get_barrier_semaphore()
-
-    def greet(a, b):
-        pl.semaphore_signal(barrier, inc=1, device_id=(a, b), device_id_type=MESH)
-
-    for_partners(greet)
+    pl.semaphore_wait(barrier, len(near) + len(beside))
+    copies = halo_copies(field, padded, halo_send, halo_recv)
+    for copy in copies:
+        copy.start()
+    signal_all(rounds.at[0], near)
     loads[0].wait()
     build_taps(1, taps, band)
     basis_inner(1, padded, band, terms.at[0])
-    pl.semaphore_wait(barrier, DEVS - 1)
-    copies = halo_copies(field, padded, halo_send, halo_recv)
-    for copy in copies:
-        copy.start()
+    pl.semaphore_wait(rounds.at[0], len(near))
+    signal_all(rounds.at[1], near)
     for load in loads[1:]:
         load.wait()
     for p, cycles in enumerate(PAIRS):
@@ -319,11 +318,16 @@
             copies[1].wait_recv()
         basis_edges(cycles[0], padded, band, terms.at[0])
         mix_terms(cycles[0], terms.at[0], mix, conv)
+        if p == 0:
+            pl.semaphore_wait(rounds.at[1], len(near))
+            signal_all(rounds.at[2], near)
         build_taps(cycles[1], taps, band)
         basis_inner(cycles[1], padded, band, terms.at[1])
         basis_edges(cycles[1], padded, band, terms.at[1])
         mix_terms(cycles[1], terms.at[1], mix, conv)
         dft_pair(p, cycles, quad, forward, conv, spectra, send)
+        if p == 0:
+            pl.semaphore_wait(rounds.at[2], len(near))
         scatter(
             p, lambda a, b: send.at[p, a * LONS + b], received, go_send.at[p], go_recv.at[p]
         )
@@ -337,18 +341,25 @@
         synth_pair(p, turned, mixed, back)
         scatter(p, lambda a, b: back.at[p, a], returned, back_send.at[p], back_recv.at[p])
         returned[p, me] = back[p, lat]
+    stores = []
     for p, cycles in enumerate(PAIRS):
         arrival(p, returned, back_send.at[p], back_recv.at[p]).wait_recv()
-        inverse_pair(p, cycles, inverse, returned, synth, conv, out)
+        inverse_pair(p, cycles, inverse, returned, synth, conv)
+        for i in cycles:
+            store = pltpu.make_async_copy(conv.at[i], out.at[i], out_sems.at[i])
+            store.start()
+            stores.append(store)
     for copy in copies:
         copy.wait_send()
     for p in range(3):
         arrival(p, received, go_send.at[p], go_recv.at[p]).wait_send()
         arrival(p, returned, back_send.at[p], back_recv.at[p]).wait_send()
-
-
+    for store in stores:
+        store.wait()
+
+
+SMEM = pl.BlockSpec(memory_space=pltpu.SMEM)
 VMEM = pl.BlockSpec(memory_space=pltpu.VMEM)
-SMEM = pl.BlockSpec(memory_space=pltpu.SMEM)
 ANY = pl.BlockSpec(memory_space=pl.ANY)
 LIMIT = 60 * 2**20
 
@@ -359,12 +370,13 @@
     return pl.pallas_call(
         kernel,
         out_shape=jax.ShapeDtypeStruct((CYCLES, HALF, C), BF16),
-        in_specs=[SMEM, SMEM, ANY, VMEM, ANY, ANY, ANY, VMEM, VMEM],
-        out_specs=VMEM,
+        in_specs=[SMEM, SMEM] + [ANY] * 7,
+        out_specs=ANY,
         scratch_shapes=[
             pltpu.VMEM((CYCLES + 2, WIDE, C), BF16),
             pltpu.VMEM((KERNELS * TILE, 3 * WINDOW), BF16),
             pltpu.VMEM((2, HALF, KERNELS * C), BF16),
+            pltpu.VMEM((KERNELS * C, C), BF16),
             pltpu.VMEM((2 * MODES, HALF), BF16),
             pltpu.VMEM((2, 2 * MODES, C), F32),
             pltpu.VMEM((CYCLES, HALF, C), BF16),
@@ -376,12 +388,16 @@
             pltpu.VMEM((3, LATS * 8, 4 * DEGREES), BF16),
             pltpu.VMEM((LATS * 8, C), BF16),
             pltpu.VMEM((4 * DEGREES, C), F32),
+            pltpu.VMEM((2, C, C), BF16),
+            pltpu.VMEM((DEGREES, C), F32),
             pltpu.VMEM((4 * DEGREES, C), BF16),
             pltpu.VMEM((3, LATS, 8, C), BF16),
             pltpu.VMEM((3, DEVS, 8, C), BF16),
             pltpu.VMEM((HALF, 2 * MODES), BF16),
             pltpu.VMEM((2, 2 * MODES, C), BF16),
-            dma((4,)),
+            pltpu.SemaphoreType.REGULAR((3,)),
+            dma((7,)),
+            dma((CYCLES,)),
             dma((8,)),
             dma((8,)),
             dma((3,)),
@@ -393,7 +409,7 @@
             collective_id=0, has_side_effects=True, vmem_limit_bytes=LIMIT
         ),
     )(
-        disco_taps.reshape(-1),
+        disco_taps,
         quad_weights,
         grid_field,
         disco_mix,

time: 134 us -> 118 us (0.88)
  Pallas kernels: 127 us -> 112 us
    pallas_call x1, Pallas kernels: 127 us -> 112 us  [body(): pl.pallas_call(kernel, out_shape=jax.ShapeDtypeStruct((CYCLES, HALF, C),...]
where the time goes in v3:
time: 118 us
  Pallas kernels  112 us (95%)
  local copies, waits for them, and re-layouts  6.23 us (5%)
    pallas_call x1, Pallas kernels, body(): pl.pallas_call(kernel, out_shape=jax.ShapeDtypeStruct((CYCLES, HALF, C),...  112 us
    unnamed x2, local copies, waits for them, and re-layouts  6.23 us

profile of v3, /device:TPU:1, one launch (start us, length us, event | category | flops | bytes accessed | tf_op | source)
XLA Modules:
  0.0 117.8 jit_solution(17070772330538774857)
XLA Ops:
  0.0 1.5 %copy.10.taps = f32[3,6,3,5]{3,2,1,0:T(4,128)} copy(f32[3,6,3,5]{1,2,3,0:T(4,128)} %param.10) | data formatting | bytes 2160 | tf_op args[1]
  1.5 111.6 %shard_map.91 = bf16[6,720,512]{2,1,0:T(8,128)(2,1)} custom-call(f32[3,6,3,5]{3,2,1,0:T(4,128)} %copy.10.taps, f32[6]{0:T(128)} %quad.1, bf16[6,720,512]{2,1,0:T(8,128)(2,1)} %field.1, bf16[1536,512]{1,0:T(8,128)(2,1)} %mix_all.1, bf16[2,512,720]{2,1,0:T(8,128)(2,1)} %constant.4.clone.forward_all, bf16[2,720,512]{2,1,0:T(8,128)(2,1)} %constant.5.clone.inverse_all, ...), custom_call_target="tpu_custom_call" | custom-call | tf_op jit(solution)/shard_map/pallas_call | solution.py:370
  113.1 4.7 %copy.12 = bf16[6,720,512]{2,1,0:T(8,128)(2,1)} copy(bf16[6,720,512]{2,1,0:T(8,128)(2,1)} %shard_map.91) | data formatting | bytes 8847360

commit v4 on v3

--- a/solution.py
+++ b/solution.py
@@ -51,7 +51,7 @@
         total = jnp.zeros((TILE, 3 * WINDOW), F32)
         for a in range(3):
             for b in range(5):
-                value = taps[k, i, a, b]
+                value = taps[k, b, a, i]
                 total = jnp.where(shift == a * WINDOW + EDGE - 2 + b, value, total)
         band[k * TILE : (k + 1) * TILE, :] = total.astype(BF16)
 
@@ -256,11 +256,11 @@
 
 
 def kernel(
-    taps, quad, field, mix_all, forward_all, inverse_all, legendre_all, weight_all, gain_all, out,
-    padded, band, terms, mix, forward, spectra, conv, send, received,
+    taps, quad, field, mix_all, forward_all, inverse_all, legendre_all, weight_all, gain_all, conv,
+    padded, band, terms, mix, forward, spectra, send, received,
     legendre, ones, table, turned, joined, coeffs, weight, gain, mixed,
     back, returned, inverse, synth,
-    rounds, local_sems, out_sems, halo_send, halo_recv, go_send, go_recv, back_send, back_recv,
+    rounds, local_sems, halo_send, halo_recv, go_send, go_recv, back_send, back_recv,
 ):
     lat, lon = lax.axis_index("lat"), lax.axis_index("lon")
     me = lat * LONS + lon
@@ -341,27 +341,20 @@
         synth_pair(p, turned, mixed, back)
         scatter(p, lambda a, b: back.at[p, a], returned, back_send.at[p], back_recv.at[p])
         returned[p, me] = back[p, lat]
-    stores = []
     for p, cycles in enumerate(PAIRS):
         arrival(p, returned, back_send.at[p], back_recv.at[p]).wait_recv()
         inverse_pair(p, cycles, inverse, returned, synth, conv)
-        for i in cycles:
-            store = pltpu.make_async_copy(conv.at[i], out.at[i], out_sems.at[i])
-            store.start()
-            stores.append(store)
     for copy in copies:
         copy.wait_send()
     for p in range(3):
         arrival(p, received, go_send.at[p], go_recv.at[p]).wait_send()
         arrival(p, returned, back_send.at[p], back_recv.at[p]).wait_send()
-    for store in stores:
-        store.wait()
 
 
 SMEM = pl.BlockSpec(memory_space=pltpu.SMEM)
 VMEM = pl.BlockSpec(memory_space=pltpu.VMEM)
 ANY = pl.BlockSpec(memory_space=pl.ANY)
-LIMIT = 60 * 2**20
+LIMIT = 59 * 2**20
 
 
 def body(grid_field, disco_taps, disco_mix, legendre, quad_weights, mix_weight, degree_gain):
@@ -369,9 +362,9 @@
     dma = pltpu.SemaphoreType.DMA
     return pl.pallas_call(
         kernel,
-        out_shape=jax.ShapeDtypeStruct((CYCLES, HALF, C), BF16),
+        out_shape=pltpu.VMEM((CYCLES, HALF, C), BF16),
         in_specs=[SMEM, SMEM] + [ANY] * 7,
-        out_specs=ANY,
+        out_specs=VMEM,
         scratch_shapes=[
             pltpu.VMEM((CYCLES + 2, WIDE, C), BF16),
             pltpu.VMEM((KERNELS * TILE, 3 * WINDOW), BF16),
@@ -379,7 +372,6 @@
             pltpu.VMEM((KERNELS * C, C), BF16),
             pltpu.VMEM((2 * MODES, HALF), BF16),
             pltpu.VMEM((2, 2 * MODES, C), F32),
-            pltpu.VMEM((CYCLES, HALF, C), BF16),
             pltpu.VMEM((3, DEVS, 8, C), BF16),
             pltpu.VMEM((3, DEVS, 8, C), BF16),
             pltpu.VMEM((2, DEGREES, LATS * CYCLES), BF16),
@@ -397,7 +389,6 @@
             pltpu.VMEM((2, 2 * MODES, C), BF16),
             pltpu.SemaphoreType.REGULAR((3,)),
             dma((7,)),
-            dma((CYCLES,)),
             dma((8,)),
             dma((8,)),
             dma((3,)),
@@ -409,7 +400,7 @@
             collective_id=0, has_side_effects=True, vmem_limit_bytes=LIMIT
         ),
     )(
-        disco_taps,
+        disco_taps.transpose(0, 3, 2, 1),
         quad_weights,
         grid_field,
         disco_mix,

time: 118 us -> 113 us (0.958)
  local copies, waits for them, and re-layouts: 6.23 us -> 2.09 us
  Pallas kernels: 112 us -> 110 us
    unnamed x2 -> x1, local copies, waits for them, and re-layouts: 6.23 us -> 2.09 us
    pallas_call x1, Pallas kernels: 112 us -> 110 us  [body(): pl.pallas_call(kernel, out_shape=pltpu.VMEM((CYCLES, HALF, C), BF16), in_...]
where the time goes in v4:
time: 113 us; the launch traced here: 112 us
  Pallas kernels  110 us (97%)
  local copies, waits for them, and re-layouts  2.09 us (2%)
    pallas_call x1, Pallas kernels, body(): pl.pallas_call(kernel, out_shape=pltpu.VMEM((CYCLES, HALF, C), BF16), in_...  110 us

profile of v4, /device:TPU:1, one launch (start us, length us, event | category | flops | bytes accessed | tf_op | source)
XLA Modules:
  0.0 112.5 jit_solution(18033388104262322049)
XLA Ops:
  0.0 110.4 %shard_map.91 = bf16[6,720,512]{2,1,0:T(8,128)(2,1)S(1)} custom-call(f32[3,5,3,6]{3,2,1,0:T(4,128)} %bitcast.1, f32[6]{0:T(128)} %quad.1, bf16[6,720,512]{2,1,0:T(8,128)(2,1)} %field.1, bf16[1536,512]{1,0:T(8,128)(2,1)} %mix_all.1, bf16[2,512,720]{2,1,0:T(8,128)(2,1)} %constant.4.clone.forward_all, bf16[2,720,512]{2,1,0:T(8,128)(2,1)} %constant.5.clone.inverse_all, ...), custom_call_target="tpu_custom_call" | custom-call | tf_op jit(solution)/shard_map/pallas_call | solution.py:363
  110.4 2.1 %copy.11 = bf16[6,720,512]{2,1,0:T(8,128)(2,1)} copy(bf16[6,720,512]{2,1,0:T(8,128)(2,1)S(1)} %shard_map.91) | data formatting | bytes 8847360

commit v5 on v4

--- a/solution.py
+++ b/solution.py
@@ -25,7 +25,8 @@
 WIDE = HALF + 2 * EDGE
 TILE = 48
 WINDOW = TILE + 2 * EDGE
-PAIRS = ((1, 2), (3, 4), (0, 5))
+INNER = (1, 2, 3, 4)
+OUTER = (0, 5)
 F32, BF16 = jnp.float32, jnp.bfloat16
 
 
@@ -80,29 +81,62 @@
         conv[i, rows, :] = dot(terms[rows, :], mix[...]).astype(BF16)
 
 
-def dft_pair(p, cycles, quad, forward, conv, spectra, send):
-    for s in range(2):
-        spectra[s] = dot(forward[...], conv[cycles[s]]) * quad[cycles[s]]
-
+def pick_rows(pieces):
+    out = None
+    for tiles, source, target in pieces:
+        turn = (target - source) % 8
+        moved = pltpu.roll(tiles, turn, 1) if turn else tiles
+        place = lax.broadcasted_iota(jnp.int32, tiles.shape, 1) // 2
+        out = moved if out is None else jnp.where(place == target // 2, moved, out)
+    return out
+
+
+def dft_cycle(s, i, quad, forward, conv, spectra):
+    spectra[s] = dot(forward[...], conv[i]) * quad[i]
+
+
+def pack_inner(spectra, send):
     @pl.loop(0, 8)
     def _(t):
         rows = pl.ds(pl.multiple_of(t * 64, 16), 64)
-        first = spectra[0, rows, :].reshape(8, 8, C)
-        second = spectra[1, rows, :].reshape(8, 8, C)
-        low = lax.broadcasted_iota(jnp.int32, (8, 8, C), 1) < 4
-        even = jnp.where(low, first, pltpu.roll(second, 4, 1))
-        odd = jnp.where(low, pltpu.roll(first, 4, 1), second)
-        both = jnp.stack([even, odd], axis=1).reshape(16, 8, C)
-        send[p, pl.ds(t * 16, 16)] = both.astype(BF16)
-
-
-def spread(p, columns_first):
+        parts = [spectra[s, rows, :].reshape(8, 8, C) for s in range(4)]
+        for m in range(2):
+            tiles = [
+                pick_rows([(parts[s], 4 * e + 2 * m, 2 * s) for s in range(4)]) for e in range(2)
+            ]
+            both = jnp.stack(tiles, axis=1).reshape(16, 8, C)
+            send[2 * m, pl.ds(t * 16, 16)] = both.astype(BF16)
+
+
+def pack_outer(spectra, send):
+    @pl.loop(0, 8)
+    def _(t):
+        rows = pl.ds(pl.multiple_of(t * 64, 16), 64)
+        parts = [spectra[s, rows, :].reshape(8, 8, C) for s in range(2)]
+        tiles = [
+            pick_rows([(parts[s], 4 * e + 2 * m, 4 * s + 2 * m) for s in range(2) for m in range(2)])
+            for e in range(2)
+        ]
+        both = jnp.stack(tiles, axis=1).reshape(16, 8, C)
+        send[1, pl.ds(t * 16, 16)] = both.astype(BF16)
+
+
+def spread(g):
     shape = (LATS * CYCLES, LATS * 8)
     cycle = lax.broadcasted_iota(jnp.int32, shape, 0)
     col = lax.broadcasted_iota(jnp.int32, shape, 1)
-    place = (col // 4) % 2
-    within = jnp.where(place == 0, PAIRS[p][0], PAIRS[p][1])
+    row = col % 8
+    within = jnp.where(row < 4, OUTER[0], OUTER[1]) if g == 1 else INNER[0] + row // 2
     return jnp.where(cycle == (col // 8) * CYCLES + within, 1.0, 0.0).astype(BF16)
+
+
+def orders_of(g):
+    return {0: (0,), 1: (0, 1), 2: (1,)}[g]
+
+
+def block_of(g):
+    orders = orders_of(g)
+    return slice(orders[0] * 2 * DEGREES, (orders[-1] + 1) * 2 * DEGREES)
 
 
 def build_triangle(first_order, legendre, ones, table, turned):
@@ -110,64 +144,85 @@
     for m in range(2):
         values = legendre[m]
         legendre[m] = jnp.where(degree >= first_order + m, values.astype(F32), 0.0).astype(BF16)
-    for p in range(3):
-        ones[...] = spread(p, False)
-        for m in range(2):
+    for g in range(3):
+        if g < 2:
+            ones[...] = spread(g)
+        else:
+            ones[...] = spread(0)
+        for m in orders_of(g):
             wide = dot(legendre[m], ones[...])
-            col = lax.broadcasted_iota(jnp.int32, wide.shape, 1) % 4
             tall = lax.dot_general(
                 ones[...], legendre[m], (((0,), (1,)), ((), ())), preferred_element_type=F32
             )
-            row = lax.broadcasted_iota(jnp.int32, tall.shape, 0) % 4
+            col = lax.broadcasted_iota(jnp.int32, wide.shape, 1)
+            row = lax.broadcasted_iota(jnp.int32, tall.shape, 0)
             for c in range(2):
                 block = slice((2 * m + c) * DEGREES, (2 * m + c + 1) * DEGREES)
-                table[p, block, :] = jnp.where(col == 2 * m + c, wide, 0.0).astype(BF16)
-                turned[p, :, block] = jnp.where(row == 2 * m + c, tall, 0.0).astype(BF16)
-
-
-def legendre_pair(p, received, joined, table, coeffs):
+                own, own_row = (
+                    (col % 4 == 2 * m + c, row % 4 == 2 * m + c)
+                    if g == 1
+                    else (col % 2 == c, row % 2 == c)
+                )
+                table[g, block, :] = jnp.where(own, wide, 0.0).astype(BF16)
+                turned[g, :, block] = jnp.where(own_row, tall, 0.0).astype(BF16)
+
+
+def legendre_group(g, received, joined, table, coeffs):
     @pl.loop(0, 8)
     def _(t):
-        block = received[p, pl.ds(t * 16, 16)].astype(F32).reshape(8, 2, 8, C)
+        block = received[g, pl.ds(t * 16, 16)].astype(F32).reshape(8, 2, 8, C)
         total = (block[:, 0] + block[:, 1]).reshape(64, C)
         joined[pl.ds(pl.multiple_of(t * 64, 16), 64), :] = total.astype(BF16)
 
-    value = dot(table[p], joined[...])
-    if p == 0:
-        coeffs[...] = value
+    if g == 0:
+        coeffs[block_of(0), :] = dot(table[0, block_of(0), :], joined[...])
+    elif g == 1:
+        coeffs[block_of(0), :] += dot(table[1, block_of(0), :], joined[...])
+        coeffs[block_of(2), :] = dot(table[1, block_of(2), :], joined[...])
     else:
-        coeffs[...] += value
-
-
-def mix_modes(coeffs, weight, gain, mixed):
-    for m in range(2):
-        real = coeffs[2 * m * DEGREES : (2 * m + 1) * DEGREES, :].astype(BF16)
-        imag = coeffs[(2 * m + 1) * DEGREES : (2 * m + 2) * DEGREES, :].astype(BF16)
-        new_real = (dot(real, weight[0]) - dot(imag, weight[1])) * gain[...]
-        mixed[2 * m * DEGREES : (2 * m + 1) * DEGREES, :] = new_real.astype(BF16)
-        new_imag = (dot(real, weight[1]) + dot(imag, weight[0])) * gain[...]
-        mixed[(2 * m + 1) * DEGREES : (2 * m + 2) * DEGREES, :] = new_imag.astype(BF16)
-
-
-def synth_pair(p, turned, mixed, send):
-    send[p] = dot(turned[p], mixed[...]).astype(BF16).reshape(LATS, 8, C)
-
-
-def inverse_pair(p, cycles, inverse, received, synth, conv):
+        coeffs[block_of(2), :] += dot(table[2, block_of(2), :], joined[...])
+
+
+def mix_modes(m, coeffs, weight, gain, mixed):
+    real = coeffs[2 * m * DEGREES : (2 * m + 1) * DEGREES, :].astype(BF16)
+    imag = coeffs[(2 * m + 1) * DEGREES : (2 * m + 2) * DEGREES, :].astype(BF16)
+    new_real = (dot(real, weight[0]) - dot(imag, weight[1])) * gain[...]
+    mixed[2 * m * DEGREES : (2 * m + 1) * DEGREES, :] = new_real.astype(BF16)
+    new_imag = (dot(real, weight[1]) + dot(imag, weight[0])) * gain[...]
+    mixed[(2 * m + 1) * DEGREES : (2 * m + 2) * DEGREES, :] = new_imag.astype(BF16)
+
+
+def synth_group(g, turned, mixed, send):
+    value = dot(turned[g, :, block_of(g)], mixed[block_of(g), :])
+    send[g] = value.astype(BF16).reshape(LATS, 8, C)
+
+
+def unpack_inner(received, synth):
     @pl.loop(0, 8)
     def _(t):
-        block = received[p, pl.ds(t * 16, 16)].astype(F32).reshape(8, 2, 8, C)
-        first, second = block[:, 0], block[:, 1]
-        low = lax.broadcasted_iota(jnp.int32, (8, 8, C), 1) < 4
+        parts = [received[2 * m, pl.ds(t * 16, 16)].astype(F32).reshape(8, 2, 8, C) for m in range(2)]
         rows = pl.ds(pl.multiple_of(t * 64, 16), 64)
-        even = jnp.where(low, first, pltpu.roll(second, 4, 1))
-        odd = jnp.where(low, pltpu.roll(first, 4, 1), second)
-        synth[0, rows, :] = even.reshape(64, C).astype(BF16)
-        synth[1, rows, :] = odd.reshape(64, C).astype(BF16)
-
-    for s in range(2):
-        value = dot(inverse[...], synth[s]) + conv[cycles[s]].astype(F32)
-        conv[cycles[s]] = value.astype(BF16)
+        for s in range(4):
+            tiles = pick_rows(
+                [(parts[m][:, e], 2 * s, 4 * e + 2 * m) for e in range(2) for m in range(2)]
+            )
+            synth[s, rows, :] = tiles.reshape(64, C).astype(BF16)
+
+
+def unpack_outer(received, synth):
+    @pl.loop(0, 8)
+    def _(t):
+        part = received[1, pl.ds(t * 16, 16)].astype(F32).reshape(8, 2, 8, C)
+        rows = pl.ds(pl.multiple_of(t * 64, 16), 64)
+        for s in range(2):
+            tiles = pick_rows(
+                [(part[:, e], 4 * s + 2 * m, 4 * e + 2 * m) for e in range(2) for m in range(2)]
+            )
+            synth[s, rows, :] = tiles.reshape(64, C).astype(BF16)
+
+
+def inverse_cycle(s, i, inverse, synth, conv):
+    conv[i] = (dot(inverse[...], synth[s]) + conv[i].astype(F32)).astype(BF16)
 
 
 def halo_copies(field, padded, send_sems, recv_sems):
@@ -297,53 +352,78 @@
     signal_all(rounds.at[1], near)
     for load in loads[1:]:
         load.wait()
-    for p, cycles in enumerate(PAIRS):
-        if p == 2:
-            for copy in copies[2:]:
-                copy.wait_recv()
-
-            @pl.when(lat == 0)
-            def _():
-                padded[0] = jnp.zeros((WIDE, C), BF16)
-
-            @pl.when(lat == LATS - 1)
-            def _():
-                padded[CYCLES + 1] = jnp.zeros((WIDE, C), BF16)
-
-        if p > 0:
-            build_taps(cycles[0], taps, band)
-            basis_inner(cycles[0], padded, band, terms.at[0])
-        else:
-            copies[0].wait_recv()
-            copies[1].wait_recv()
-        basis_edges(cycles[0], padded, band, terms.at[0])
-        mix_terms(cycles[0], terms.at[0], mix, conv)
-        if p == 0:
+    copies[0].wait_recv()
+    copies[1].wait_recv()
+    for s, i in enumerate(INNER):
+        store = terms.at[s % 2]
+        if s > 0:
+            build_taps(i, taps, band)
+            basis_inner(i, padded, band, store)
+        basis_edges(i, padded, band, store)
+        mix_terms(i, store, mix, conv)
+        if s == 0:
             pl.semaphore_wait(rounds.at[1], len(near))
             signal_all(rounds.at[2], near)
-        build_taps(cycles[1], taps, band)
-        basis_inner(cycles[1], padded, band, terms.at[1])
-        basis_edges(cycles[1], padded, band, terms.at[1])
-        mix_terms(cycles[1], terms.at[1], mix, conv)
-        dft_pair(p, cycles, quad, forward, conv, spectra, send)
-        if p == 0:
-            pl.semaphore_wait(rounds.at[2], len(near))
+        dft_cycle(s, i, quad, forward, conv, spectra)
+    pack_inner(spectra, send)
+    pl.semaphore_wait(rounds.at[2], len(near))
+
+    def go(g):
         scatter(
-            p, lambda a, b: send.at[p, a * LONS + b], received, go_send.at[p], go_recv.at[p]
+            g, lambda a, b: send.at[g, a * LONS + b], received, go_send.at[g], go_recv.at[g]
         )
-        received[p, me] = send[p, me]
+        received[g, me] = send[g, me]
+
+    go(0)
+    for copy in copies[2:]:
+        copy.wait_recv()
+
+    @pl.when(lat == 0)
+    def _():
+        padded[0] = jnp.zeros((WIDE, C), BF16)
+
+    @pl.when(lat == LATS - 1)
+    def _():
+        padded[CYCLES + 1] = jnp.zeros((WIDE, C), BF16)
+
+    for s, i in enumerate(OUTER):
+        store = terms.at[s]
+        build_taps(i, taps, band)
+        basis_inner(i, padded, band, store)
+        basis_edges(i, padded, band, store)
+        mix_terms(i, store, mix, conv)
+        dft_cycle(s, i, quad, forward, conv, spectra)
+    pack_outer(spectra, send)
+    go(1)
+    go(2)
     build_triangle(4 * lat + 2 * lon, legendre, ones, table, turned)
-    for p in range(3):
-        arrival(p, received, go_send.at[p], go_recv.at[p]).wait_recv()
-        legendre_pair(p, received, joined, table, coeffs)
-    mix_modes(coeffs, weight, gain, mixed)
-    for p in range(3):
-        synth_pair(p, turned, mixed, back)
-        scatter(p, lambda a, b: back.at[p, a], returned, back_send.at[p], back_recv.at[p])
-        returned[p, me] = back[p, lat]
-    for p, cycles in enumerate(PAIRS):
-        arrival(p, returned, back_send.at[p], back_recv.at[p]).wait_recv()
-        inverse_pair(p, cycles, inverse, returned, synth, conv)
+
+    def take(g):
+        arrival(g, received, go_send.at[g], go_recv.at[g]).wait_recv()
+        legendre_group(g, received, joined, table, coeffs)
+
+    def give(g):
+        synth_group(g, turned, mixed, back)
+        scatter(g, lambda a, b: back.at[g, a], returned, back_send.at[g], back_recv.at[g])
+        returned[g, me] = back[g, lat]
+
+    take(0)
+    take(1)
+    mix_modes(0, coeffs, weight, gain, mixed)
+    give(0)
+    take(2)
+    mix_modes(1, coeffs, weight, gain, mixed)
+    give(2)
+    give(1)
+    for g in (0, 2):
+        arrival(g, returned, back_send.at[g], back_recv.at[g]).wait_recv()
+    unpack_inner(returned, synth)
+    for s, i in enumerate(INNER):
+        inverse_cycle(s, i, inverse, synth, conv)
+    arrival(1, returned, back_send.at[1], back_recv.at[1]).wait_recv()
+    unpack_outer(returned, synth)
+    for s, i in enumerate(OUTER):
+        inverse_cycle(s, i, inverse, synth, conv)
     for copy in copies:
         copy.wait_send()
     for p in range(3):
@@ -371,7 +451,7 @@
             pltpu.VMEM((2, HALF, KERNELS * C), BF16),
             pltpu.VMEM((KERNELS * C, C), BF16),
             pltpu.VMEM((2 * MODES, HALF), BF16),
-            pltpu.VMEM((2, 2 * MODES, C), F32),
+            pltpu.VMEM((4, 2 * MODES, C), F32),
             pltpu.VMEM((3, DEVS, 8, C), BF16),
             pltpu.VMEM((3, DEVS, 8, C), BF16),
             pltpu.VMEM((2, DEGREES, LATS * CYCLES), BF16),
@@ -386,7 +466,7 @@
             pltpu.VMEM((3, LATS, 8, C), BF16),
             pltpu.VMEM((3, DEVS, 8, C), BF16),
             pltpu.VMEM((HALF, 2 * MODES), BF16),
-            pltpu.VMEM((2, 2 * MODES, C), BF16),
+            pltpu.VMEM((4, 2 * MODES, C), BF16),
             pltpu.SemaphoreType.REGULAR((3,)),
             dma((7,)),
             dma((8,)),

time: 113 us -> 111 us (0.982)
    pallas_call x1, Pallas kernels: 110 us -> 109 us  [body(): pl.pallas_call(kernel, out_shape=pltpu.VMEM((CYCLES, HALF, C), BF16), in_...]
where the time goes in v5:
time: 111 us
  Pallas kernels  109 us (98%)
  local copies, waits for them, and re-layouts  2.09 us (2%)
    pallas_call x1, Pallas kernels, body(): pl.pallas_call(kernel, out_shape=pltpu.VMEM((CYCLES, HALF, C), BF16), in_...  109 us

profile of v5, /device:TPU:1, one launch (start us, length us, event | category | flops | bytes accessed | tf_op | source)
XLA Modules:
  0.0 111.3 jit_solution(15233022323212668523)
XLA Ops:
  0.0 109.2 %shard_map.91 = bf16[6,720,512]{2,1,0:T(8,128)(2,1)S(1)} custom-call(f32[3,5,3,6]{3,2,1,0:T(4,128)} %bitcast.1, f32[6]{0:T(128)} %quad.1, bf16[6,720,512]{2,1,0:T(8,128)(2,1)} %field.1, bf16[1536,512]{1,0:T(8,128)(2,1)} %mix_all.1, bf16[2,512,720]{2,1,0:T(8,128)(2,1)} %constant.4.clone.forward_all, bf16[2,720,512]{2,1,0:T(8,128)(2,1)} %constant.5.clone.inverse_all, ...), custom_call_target="tpu_custom_call" | custom-call | tf_op jit(solution)/shard_map/pallas_call | solution.py:443
  109.2 2.1 %copy.11 = bf16[6,720,512]{2,1,0:T(8,128)(2,1)} copy(bf16[6,720,512]{2,1,0:T(8,128)(2,1)S(1)} %shard_map.91) | data formatting | bytes 8847360

commit v6 on v5

--- a/solution.py
+++ b/solution.py
@@ -25,8 +25,8 @@
 WIDE = HALF + 2 * EDGE
 TILE = 48
 WINDOW = TILE + 2 * EDGE
-INNER = (1, 2, 3, 4)
-OUTER = (0, 5)
+QUAD = (3, 4, 0, 5)
+PAIR = (1, 2)
 F32, BF16 = jnp.float32, jnp.bfloat16
 
 
@@ -126,7 +126,11 @@
     cycle = lax.broadcasted_iota(jnp.int32, shape, 0)
     col = lax.broadcasted_iota(jnp.int32, shape, 1)
     row = col % 8
-    within = jnp.where(row < 4, OUTER[0], OUTER[1]) if g == 1 else INNER[0] + row // 2
+    if g == 1:
+        within = jnp.where(row < 4, PAIR[0], PAIR[1])
+    else:
+        late = jnp.where(row < 6, QUAD[2], QUAD[3])
+        within = jnp.where(row < 2, QUAD[0], jnp.where(row < 4, QUAD[1], late))
     return jnp.where(cycle == (col // 8) * CYCLES + within, 1.0, 0.0).astype(BF16)
 
 
@@ -174,13 +178,11 @@
         total = (block[:, 0] + block[:, 1]).reshape(64, C)
         joined[pl.ds(pl.multiple_of(t * 64, 16), 64), :] = total.astype(BF16)
 
-    if g == 0:
-        coeffs[block_of(0), :] = dot(table[0, block_of(0), :], joined[...])
-    elif g == 1:
-        coeffs[block_of(0), :] += dot(table[1, block_of(0), :], joined[...])
-        coeffs[block_of(2), :] = dot(table[1, block_of(2), :], joined[...])
+    value = dot(table[g, block_of(g), :], joined[...])
+    if g == 1:
+        coeffs[...] = value
     else:
-        coeffs[block_of(2), :] += dot(table[2, block_of(2), :], joined[...])
+        coeffs[block_of(g), :] += value
 
 
 def mix_modes(m, coeffs, weight, gain, mixed):
@@ -354,19 +356,6 @@
         load.wait()
     copies[0].wait_recv()
     copies[1].wait_recv()
-    for s, i in enumerate(INNER):
-        store = terms.at[s % 2]
-        if s > 0:
-            build_taps(i, taps, band)
-            basis_inner(i, padded, band, store)
-        basis_edges(i, padded, band, store)
-        mix_terms(i, store, mix, conv)
-        if s == 0:
-            pl.semaphore_wait(rounds.at[1], len(near))
-            signal_all(rounds.at[2], near)
-        dft_cycle(s, i, quad, forward, conv, spectra)
-    pack_inner(spectra, send)
-    pl.semaphore_wait(rounds.at[2], len(near))
 
     def go(g):
         scatter(
@@ -374,7 +363,24 @@
         )
         received[g, me] = send[g, me]
 
-    go(0)
+    def convolve(s, i, ready):
+        store = terms.at[s % 2]
+        if not ready:
+            build_taps(i, taps, band)
+            basis_inner(i, padded, band, store)
+        basis_edges(i, padded, band, store)
+        mix_terms(i, store, mix, conv)
+        dft_cycle(s, i, quad, forward, conv, spectra)
+
+    convolve(0, PAIR[0], True)
+    pl.semaphore_wait(rounds.at[1], len(near))
+    signal_all(rounds.at[2], near)
+    convolve(1, PAIR[1], False)
+    pack_outer(spectra, send)
+    pl.semaphore_wait(rounds.at[2], len(near))
+    go(1)
+    convolve(0, QUAD[0], False)
+    convolve(1, QUAD[1], False)
     for copy in copies[2:]:
         copy.wait_recv()
 
@@ -386,15 +392,10 @@
     def _():
         padded[CYCLES + 1] = jnp.zeros((WIDE, C), BF16)
 
-    for s, i in enumerate(OUTER):
-        store = terms.at[s]
-        build_taps(i, taps, band)
-        basis_inner(i, padded, band, store)
-        basis_edges(i, padded, band, store)
-        mix_terms(i, store, mix, conv)
-        dft_cycle(s, i, quad, forward, conv, spectra)
-    pack_outer(spectra, send)
-    go(1)
+    convolve(2, QUAD[2], False)
+    convolve(3, QUAD[3], False)
+    pack_inner(spectra, send)
+    go(0)
     go(2)
     build_triangle(4 * lat + 2 * lon, legendre, ones, table, turned)
 
@@ -407,8 +408,8 @@
         scatter(g, lambda a, b: back.at[g, a], returned, back_send.at[g], back_recv.at[g])
         returned[g, me] = back[g, lat]
 
+    take(1)
     take(0)
-    take(1)
     mix_modes(0, coeffs, weight, gain, mixed)
     give(0)
     take(2)
@@ -418,11 +419,11 @@
     for g in (0, 2):
         arrival(g, returned, back_send.at[g], back_recv.at[g]).wait_recv()
     unpack_inner(returned, synth)
-    for s, i in enumerate(INNER):
+    for s, i in enumerate(QUAD):
         inverse_cycle(s, i, inverse, synth, conv)
     arrival(1, returned, back_send.at[1], back_recv.at[1]).wait_recv()
     unpack_outer(returned, synth)
-    for s, i in enumerate(OUTER):
+    for s, i in enumerate(PAIR):
         inverse_cycle(s, i, inverse, synth, conv)
     for copy in copies:
         copy.wait_send()

time: 111 us -> 112 us (level)
  no operation moved by 1% of the time
where the time goes in v6:
time: 112 us
  Pallas kernels  110 us (98%)
  local copies, waits for them, and re-layouts  2.09 us (2%)
    pallas_call x1, Pallas kernels, body(): pl.pallas_call(kernel, out_shape=pltpu.VMEM((CYCLES, HALF, C), BF16), in_...  110 us

profile of v6, /device:TPU:1, one launch (start us, length us, event | category | flops | bytes accessed | tf_op | source)
XLA Modules:
  0.0 111.8 jit_solution(14767479451255914955)
XLA Ops:
  0.0 109.7 %shard_map.91 = bf16[6,720,512]{2,1,0:T(8,128)(2,1)S(1)} custom-call(f32[3,5,3,6]{3,2,1,0:T(4,128)} %bitcast.1, f32[6]{0:T(128)} %quad.1, bf16[6,720,512]{2,1,0:T(8,128)(2,1)} %field.1, bf16[1536,512]{1,0:T(8,128)(2,1)} %mix_all.1, bf16[2,512,720]{2,1,0:T(8,128)(2,1)} %constant.4.clone.forward_all, bf16[2,720,512]{2,1,0:T(8,128)(2,1)} %constant.5.clone.inverse_all, ...), custom_call_target="tpu_custom_call" | custom-call | tf_op jit(solution)/shard_map/pallas_call | solution.py:444
  109.7 2.1 %copy.11 = bf16[6,720,512]{2,1,0:T(8,128)(2,1)} copy(bf16[6,720,512]{2,1,0:T(8,128)(2,1)S(1)} %shard_map.91) | data formatting | bytes 8847360

commit v7 on v5

--- a/solution.py
+++ b/solution.py
@@ -19,7 +19,7 @@
 LONS = 2
 DEVS = LATS * LONS
 CHIPS = 64
-STRIDE = 43
+STRIDE = 27
 HALF = NLON // LONS
 EDGE = 16
 WIDE = HALF + 2 * EDGE

time: 111 us -> 110 us (level)
    pallas_call x1, Pallas kernels: 109 us -> 108 us  [body(): pl.pallas_call(kernel, out_shape=pltpu.VMEM((CYCLES, HALF, C), BF16), in_...]
where the time goes in v7:
time: 110 us
  Pallas kernels  108 us (98%)
  local copies, waits for them, and re-layouts  2.09 us (2%)
    pallas_call x1, Pallas kernels, body(): pl.pallas_call(kernel, out_shape=pltpu.VMEM((CYCLES, HALF, C), BF16), in_...  108 us

profile of v7, /device:TPU:1, one launch (start us, length us, event | category | flops | bytes accessed | tf_op | source)
XLA Modules:
  0.0 110.0 jit_solution(10549065963367073748)
XLA Ops:
  0.0 107.9 %shard_map.91 = bf16[6,720,512]{2,1,0:T(8,128)(2,1)S(1)} custom-call(f32[3,5,3,6]{3,2,1,0:T(4,128)} %bitcast.1, f32[6]{0:T(128)} %quad.1, bf16[6,720,512]{2,1,0:T(8,128)(2,1)} %field.1, bf16[1536,512]{1,0:T(8,128)(2,1)} %mix_all.1, bf16[2,512,720]{2,1,0:T(8,128)(2,1)} %constant.4.clone.forward_all, bf16[2,720,512]{2,1,0:T(8,128)(2,1)} %constant.5.clone.inverse_all, ...), custom_call_target="tpu_custom_call" | custom-call | tf_op jit(solution)/shard_map/pallas_call | solution.py:443
  108.0 2.1 %copy.11 = bf16[6,720,512]{2,1,0:T(8,128)(2,1)} copy(bf16[6,720,512]{2,1,0:T(8,128)(2,1)S(1)} %shard_map.91) | data formatting | bytes 8847360
